TPU v7x, 512 devices: a whole 4x8x8 slice. The times are simulated.
512 devices in a mesh: flow: 128 (over y, z, core), tp: 4 (over x).
Axes of the slice: x: 4, y: 8, z: 8, core: 2. Of those that a mesh axis runs over, the one named last changes fastest.
Arguments:
- packets: bfloat16 [32768, 1024], P('flow', 'tp'), may hold values from -6 to 6
- packet_flow: int32 [32768], P('flow'), may hold values from 0 to 255, as said below
- packet_pos: int32 [32768], P('flow'), may hold values from 0 to 638, as said below
- flow_holder_rank: int32 [256], replicated, may hold values from 0 to 127, as said below
- flow_first_block: int32 [256], replicated, may hold values from 0 to 5, as said below
- w_qkv: bfloat16 [3, 1024, 1024], P(None, None, 'tp'), may hold values from -0.1875 to 0.1875
- w_out: bfloat16 [1024, 1024], P('tp'), may hold values from -0.1875 to 0.1875
- w_up: bfloat16 [1024, 2048], P(None, 'tp'), may hold values from -0.1875 to 0.1875
- w_down: bfloat16 [2048, 1024], P('tp'), may hold values from -0.125 to 0.125
- gain_first: bfloat16 [1024], P('tp'), may hold values from 0.5 to 1.5
- gain_second: bfloat16 [1024], P('tp'), may hold values from 0.5 to 1.5
- head_slopes: float32 [16], P('tp'), may hold values from 0.002 to 0.3
Outputs:
- encoded: bfloat16 [32768, 1024], P('flow', 'tp')
- context: bfloat16 [32768, 1024], P('flow', 'tp')
Inputs may be any that keep to these rules, and one draw needn't show every extreme that they name: `packet_flow`: each flow has 1 to 639 packets. `packet_pos`: the packets of one flow carry the positions 0 to its length - 1, once each, rising with capture time (index of flow, then row). `flow_holder_rank`: each owner holds exactly two flows. At most 5 packets of one index of flow belong to the flows of one owner, and some index sends exactly 5 to some owner. `flow_first_block`: an owner's first flow starts at block 0 and its second right after the first flow's blocks; each flow's packets fit within its blocks of 128 slots; an owner's two flows take at most 6 blocks, and some owner takes all of them.
All inputs are finite; a program needn't handle non-finite values.
Results may differ from a plain program's by a relative error of at most 0.017.
Values may be sent and summed in bfloat16 or wider, within the bound.
A program may use at most 64 MiB of HBM per device.

v0:
```python
import jax
import jax.numpy as jnp
from jax import lax
from jax.sharding import PartitionSpec as P

D = 1024
BLOCK = 128
HEAD_DIM = 64


EPS = 1e-05
DIGIT = 128


def norm_apply(values, total, square, gain):
    mean = total / D
    spread = square / D - mean * mean
    return ((values - mean) * lax.rsqrt(spread + EPS) * gain.astype(jnp.float32)).astype(
        jnp.bfloat16
    )


def normalize(rows, gain):
    values = rows.astype(jnp.float32)
    total, square = lax.psum(
        (jnp.sum(values, axis=1, keepdims=True), jnp.sum(values * values, axis=1, keepdims=True)),
        "tp",
    )
    return norm_apply(values, total, square, gain)


def on_device(
    packets,
    packet_flow,
    packet_pos,
    flow_holder_rank,
    flow_first_block,
    w_qkv,
    w_out,
    w_up,
    w_down,
    gain_first,
    gain_second,
    head_slopes,
):
    owners = lax.axis_size("flow")
    myself = lax.axis_index("flow")
    count_here = packets.shape[0]
    local_width = packets.shape[1]
    per_shard = count_here // BLOCK
    nblocks = 4 * per_shard - 2
    slots = nblocks * BLOCK
    capacity = (BLOCK * (nblocks - 1) + owners - 1) // owners
    flows = flow_holder_rank.shape[0]
    flow_ids = lax.broadcasted_iota(jnp.int32, (count_here, flows), 1)
    pick = packet_flow[:, None] == flow_ids
    dest = jnp.sum(jnp.where(pick, flow_holder_rank[None, :], 0), axis=1)
    start = jnp.sum(jnp.where(pick, flow_first_block[None, :], 0), axis=1)
    slot = start * BLOCK + packet_pos
    rows_iota = lax.broadcasted_iota(jnp.int32, (count_here, count_here), 0)
    cols_iota = lax.broadcasted_iota(jnp.int32, (count_here, count_here), 1)
    before = (dest[:, None] == dest[None, :]) & (rows_iota > cols_iota)
    rank = jnp.sum(before.astype(jnp.int32), axis=1)
    send_row = dest * capacity + rank
    code = slot + 1
    digits = jnp.stack([code // DIGIT, code % DIGIT], axis=1).astype(jnp.bfloat16)
    outbox = jnp.zeros((owners * capacity, local_width), jnp.bfloat16).at[send_row].set(packets)
    outcodes = jnp.zeros((owners * capacity, 2), jnp.bfloat16).at[send_row].set(digits)
    inbox, incodes = (
        lax.all_to_all(outbox, "flow", split_axis=0, concat_axis=0, tiled=True),
        lax.all_to_all(outcodes, "flow", split_axis=0, concat_axis=0, tiled=True),
    )
    got = incodes.astype(jnp.int32)
    code_in = got[:, 0] * DIGIT + got[:, 1]
    target = jnp.where(code_in > 0, code_in - 1, slots)
    buffer = jnp.zeros((slots + 1, local_width), jnp.bfloat16).at[target].set(inbox)[:slots]
    filled = jnp.zeros((slots + 1,), jnp.float32).at[target].set(1.0)[:slots]
    second_start = jnp.max(jnp.where(flow_holder_rank == myself, flow_first_block, 0))
    place = jnp.arange(slots, dtype=jnp.int32)
    tag = (place >= second_start * BLOCK).astype(jnp.int32)
    normed = normalize(buffer, gain_first)
    weight_rows = w_qkv
    qkv = jnp.einsum(
        "sd,kdc->ksc",
        lax.all_gather(normed, "tp", axis=1, tiled=True),
        weight_rows,
        preferred_element_type=jnp.float32,
    )
    qkv = qkv.astype(jnp.bfloat16)
    heads_here = local_width // HEAD_DIM
    scale = HEAD_DIM ** (-0.5)

    def head_major(part):
        return part.reshape(slots, heads_here, HEAD_DIM).transpose(1, 0, 2)

    distance = jnp.abs(place[:, None] - place[None, :]).astype(jnp.float32)
    allowed = (tag[:, None] == tag[None, :]) & (filled[None, :] > 0) | (
        place[:, None] == place[None, :]
    )

    def one_head(inputs):
        query, key_rows, value_rows, slope = inputs
        scores = (
            lax.dot_general(
                query, key_rows, (((1,), (1,)), ((), ())), preferred_element_type=jnp.float32
            )
            * scale
            - slope * distance
        )
        weights = jnp.where(allowed, jnp.exp(scores), 0.0)
        probs = (weights / jnp.sum(weights, axis=1, keepdims=True)).astype(jnp.bfloat16)
        return jnp.dot(probs, value_rows, preferred_element_type=jnp.float32).astype(jnp.bfloat16)

    mixed = lax.map(
        one_head, (head_major(qkv[0]), head_major(qkv[1]), head_major(qkv[2]), head_slopes)
    )
    attended = mixed.transpose(1, 0, 2).reshape(slots, local_width)
    attn_terms = jnp.dot(attended, w_out, preferred_element_type=jnp.float32)
    attn_out = lax.psum_scatter(
        attn_terms.astype(jnp.bfloat16), "tp", scatter_dimension=1, tiled=True
    ).astype(jnp.float32)
    middle = (buffer.astype(jnp.float32) + attn_out).astype(jnp.bfloat16)
    normed_second = normalize(middle, gain_second)
    weight_rows = w_up
    upward = jnp.dot(
        lax.all_gather(normed_second, "tp", axis=1, tiled=True),
        weight_rows,
        preferred_element_type=jnp.float32,
    )
    active = jax.nn.gelu(upward, approximate=False).astype(jnp.bfloat16)
    down_terms = jnp.dot(active, w_down, preferred_element_type=jnp.float32)
    mlp_out = lax.psum_scatter(
        down_terms.astype(jnp.bfloat16), "tp", scatter_dimension=1, tiled=True
    ).astype(jnp.float32)
    encoded_slots = (middle.astype(jnp.float32) + mlp_out).astype(jnp.bfloat16)
    members = jnp.stack([(tag == 0) & (filled > 0), (tag == 1) & (filled > 0)]).astype(jnp.bfloat16)
    totals = jnp.dot(members, encoded_slots, preferred_element_type=jnp.float32)
    counts = jnp.sum(members.astype(jnp.float32), axis=1, keepdims=True)
    pooled = (totals / counts).astype(jnp.bfloat16)
    padded_rows = jnp.concatenate(
        [encoded_slots, jnp.zeros((1, local_width), jnp.bfloat16)], axis=0
    )
    reply = padded_rows[target]
    slot_tag = jnp.concatenate([tag, jnp.zeros((1,), jnp.int32)], axis=0)[target]
    context_rows = jnp.where(slot_tag[:, None] == 1, pooled[1][None, :], pooled[0][None, :])
    back, back_context = (
        lax.all_to_all(reply, "flow", split_axis=0, concat_axis=0, tiled=True),
        lax.all_to_all(context_rows, "flow", split_axis=0, concat_axis=0, tiled=True),
    )
    context = back_context[send_row]
    encoded = back[send_row]
    return (encoded, context)


def solution(mesh):
    return jax.shard_map(
        on_device,
        mesh=mesh,
        in_specs=(
            P("flow", "tp"),
            P("flow"),
            P("flow"),
            P(),
            P(),
            P(None, None, "tp"),
            P("tp", None),
            P(None, "tp"),
            P("tp", None),
            P("tp"),
            P("tp"),
            P("tp"),
        ),
        out_specs=(P("flow", "tp"), P("flow", "tp")),
        check_vma=False,
    )
```

profile of v0, /device:TPU:1, one launch (start us, length us, event | category | flops | bytes accessed | tf_op | source)
XLA Modules:
  0.0 334.9 jit_solution(2217142283399336136)
XLA Ops:
  7.2 1.1 select_reduce_fusion
  9.3 1.2 scatter_custom_fusion
  11.6 18.4 %all-to-all-start = ((bf16[128,5,2]{1,2,0:T(2,128)(2,1)}), bf16[128,5,2]{1,2,0:T(2,128)(2,1)S(1)}, u32[]{:S(2)}, u32[]{:S(2)}) async-start(bf16[128,5,2]{1,2,0:T(2,128)(2,1)} %copy.46), calls=%async_computation | async-start | bytes 131072 | tf_op jit(solution)/shard_map/all_to_all | solution.py:71
  30.1 1.9 scatter_custom_fusion.1
  32.0 0.9 all_to_all.30
  32.9 8.6 %all-to-all-done = bf16[128,5,2]{1,2,0:T(2,128)(2,1)S(1)} async-done(((bf16[128,5,2]{1,2,0:T(2,128)(2,1)}), bf16[128,5,2]{1,2,0:T(2,128)(2,1)S(1)}, u32[]{:S(2)}, u32[]{:S(2)}) %all-to-all-start) | async-done | bytes 2592 | tf_op jit(solution)/shard_map/all_to_all | solution.py:71
  41.5 5.7 %all-to-all-start.1 = ((bf16[128,5,256]{2,1,0:T(8,128)(2,1)}), bf16[128,5,256]{2,1,0:T(8,128)(2,1)S(1)}, u32[]{:S(2)}, u32[]{:S(2)}) async-start(bf16[128,5,256]{2,1,0:T(8,128)(2,1)} %all_to_all.30), calls=%async_computation.1 | async-start | bytes 1048576 | tf_op jit(solution)/shard_map/all_to_all | solution.py:70
  47.8 19.0 %all-to-all-done.1 = bf16[128,5,256]{2,1,0:T(8,128)(2,1)S(1)} async-done(((bf16[128,5,256]{2,1,0:T(8,128)(2,1)}), bf16[128,5,256]{2,1,0:T(8,128)(2,1)S(1)}, u32[]{:S(2)}, u32[]{:S(2)}) %all-to-all-start.1) | async-done | bytes 327712 | tf_op jit(solution)/shard_map/all_to_all | solution.py:70
  67.0 5.4 %scatter_custom_fusion.2 = bf16[769,256]{1,0:T(8,128)(2,1)S(1)} fusion(s32[640]{0:T(1024)S(1)} %fusion.88, bf16[640,256]{1,0:T(8,128)(2,1)S(1)} %reshape.140, bf16[]{:T(256)} %constant.57.clone.1), kind=kCustom, calls=%fused_computation.111 | custom fusion | bytes 393730 | tf_op jit(solution)/shard_map/scatter | solution.py:76
  72.7 8.6 %all-reduce.2 = (f32[768,1]{0,1:T(1,128)S(1)}, f32[768,1]{0,1:T(1,128)S(1)}) all-reduce(f32[768,1]{0,1:T(1,128)S(1)} %broadcast_in_dim.124, f32[768,1]{0,1:T(1,128)S(1)} %broadcast_in_dim.125), channel_id=1, replica_groups=mesh['flow'=128,'tp'=4] {'tp'}, use_global_device_ids=true, to_apply=%region_7.8 | all-reduce | flops 1536 | bytes 12288 | tf_op jit(solution)/shard_map/psum | solution.py:25
  81.3 1.0 fusion.42
  83.8 4.3 %scatter_custom_fusion.3 = f32[769]{0:T(1024)S(1)} fusion(s32[640]{0:T(1024)S(1)} %fusion.88, f32[640]{0:T(1024)S(1)} %broadcast.122, f32[]{:T(128)} %constant.34.clone.1), kind=kCustom, calls=%fused_computation.136 | custom fusion | bytes 3080 | tf_op jit(solution)/shard_map/scatter | solution.py:77
  88.6 22.0 %all-gather.3.cloned.1.call-done = bf16[768,1024]{1,0:T(8,128)(2,1)} async-done(((bf16[768,256]{1,0:T(8,128)(2,1)}), bf16[768,1024]{1,0:T(8,128)(2,1)}) %all-gather.3.cloned.1.call-update) | async-done | bytes 1572880 | tf_op jit(solution)/shard_map/all_gather | solution.py:85
  110.7 2.8 fusion.35
  113.6 1.2 copy.50
  115.1 1.2 copy.52
  116.3 24.9 %while.11 = (s32[]{:T(128)}, bf16[4,768,64]{1,2,0:T(8,128)(2,1)}, bf16[4,768,64]{2,1,0:T(8,128)(2,1)}, bf16[4,768,64]{2,1,0:T(8,128)(2,1)S(1)}, f32[4]{0:T(128)}...) while((s32[]{:T(128)}, bf16[4,768,64]{1,2,0:T(8,128)(2,1)}, ...), condition=%wide.region_14.15_spmd.clone, body=%wide.region_12.14_spmd.clone.sunk | while | flops 159300864 | bytes 5424745 | solution.py:114
  116.3 1.3 dynamic_slice.41
  117.6 3.0 fusion.141
  120.6 1.9 fusion.142
  122.6 1.3 dynamic_slice.41
  123.8 3.0 fusion.141
  126.8 1.9 fusion.142
  128.8 1.3 dynamic_slice.41
  130.0 3.0 fusion.141
  133.0 2.0 fusion.142
  135.0 1.3 dynamic_slice.41
  136.2 3.0 fusion.141
  139.2 1.9 fusion.142
  141.2 2.8 convolution_convert_fusion.1
  144.1 32.0 %reduce-scatter.3.cloned.1.call-done = bf16[768,256]{1,0:T(8,128)(2,1)} async-done(((bf16[768,1024]{1,0:T(8,128)(2,1)}), bf16[768,256]{1,0:T(8,128)(2,1)}) %reduce-scatter.3.cloned.1.call-update) | async-done | bytes 393232 | tf_op jit(solution)/shard_map/reduce_scatter | solution.py:119
  176.1 1.3 convert_reduce_fusion
  177.4 7.4 %all-reduce.1 = (f32[768,1]{0,1:T(1,128)S(1)}, f32[768,1]{0,1:T(1,128)S(1)}) all-reduce(f32[768,1]{0,1:T(1,128)S(1)} %broadcast_in_dim.128, f32[768,1]{0,1:T(1,128)S(1)} %broadcast_in_dim.129), channel_id=1, replica_groups=mesh['flow'=128,'tp'=4] {'tp'}, use_global_device_ids=true, to_apply=%region_17.18 | all-reduce | flops 1536 | bytes 12288 | tf_op jit(solution)/shard_map/psum | solution.py:25
  184.9 1.0 fusion.47
  186.0 36.6 %all-gather.5.cloned.1.call-done = bf16[768,1024]{1,0:T(8,128)(2,1)} async-done(((bf16[768,256]{1,0:T(8,128)(2,1)}), bf16[768,1024]{1,0:T(8,128)(2,1)}) %all-gather.5.cloned.1.call-update) | async-done | bytes 1572880 | tf_op jit(solution)/shard_map/all_gather | solution.py:126
  222.5 7.8 %convolution_convert_fusion = bf16[768,1024]{1,0:T(8,128)(2,1)} fusion(bf16[512,1024]{1,0:T(8,128)(2,1)S(1)} %copy-done.6, bf16[768,1024]{1,0:T(8,128)(2,1)} %all-gather.5.cloned.1.call-done, bf16[1024,512]{1,0:T(8,128)(2,1)} %param.21), kind=kOutput, calls=%fused_computation.30 | convolution fusion | flops 1636958208 | bytes 5242880 | tf_op jit(solution)/shard_map/dot_general | solution.py:131
  231.1 2.8 gather_fusion.2
  234.3 28.2 %reduce-scatter.5.cloned.1.call-done = bf16[768,256]{1,0:T(8,128)(2,1)} async-done(((bf16[768,1024]{1,0:T(8,128)(2,1)}), bf16[768,256]{1,0:T(8,128)(2,1)}) %reduce-scatter.5.cloned.1.call-update) | async-done | bytes 393232 | tf_op jit(solution)/shard_map/reduce_scatter | solution.py:132
  262.5 1.1 fusion.49
  263.8 1.0 broadcast_select_fusion
  264.8 15.3 %all-to-all-start.3 = ((bf16[128,5,256]{2,1,0:T(8,128)(2,1)}), bf16[128,5,256]{2,1,0:T(8,128)(2,1)S(1)}, u32[]{:S(2)}, u32[]{:S(2)}) async-start(bf16[128,5,256]{2,1,0:T(8,128)(2,1)} %broadcast_select_fusion), calls=%async_computation.5 | async-start | bytes 1048576 | tf_op jit(solution)/shard_map/all_to_all | solution.py:148
  280.1 2.8 gather_fusion
  282.9 0.9 all_to_all.33
  283.8 15.7 %all-to-all-done.3 = bf16[128,5,256]{2,1,0:T(8,128)(2,1)S(1)} async-done(((bf16[128,5,256]{2,1,0:T(8,128)(2,1)}), bf16[128,5,256]{2,1,0:T(8,128)(2,1)S(1)}, u32[]{:S(2)}, u32[]{:S(2)}) %all-to-all-start.3) | async-done | bytes 327712 | tf_op jit(solution)/shard_map/all_to_all | solution.py:148
  299.6 7.2 %all-to-all-start.2 = ((bf16[128,5,256]{2,1,0:T(8,128)(2,1)}), bf16[128,5,256]{2,1,0:T(8,128)(2,1)S(1)}, u32[]{:S(2)}, u32[]{:S(2)}) async-start(bf16[128,5,256]{2,1,0:T(8,128)(2,1)} %all_to_all.33), calls=%async_computation.4 | async-start | bytes 1048576 | tf_op jit(solution)/shard_map/all_to_all | solution.py:147
  307.0 1.8 gather_fusion.3
  308.8 17.6 %all-to-all-done.2 = bf16[128,5,256]{2,1,0:T(8,128)(2,1)S(1)} async-done(((bf16[128,5,256]{2,1,0:T(8,128)(2,1)}), bf16[128,5,256]{2,1,0:T(8,128)(2,1)S(1)}, u32[]{:S(2)}, u32[]{:S(2)}) %all-to-all-start.2) | async-done | bytes 327712 | tf_op jit(solution)/shard_map/all_to_all | solution.py:147
  326.5 1.8 gather_fusion.1
  (72 shorter events, 6.6 us)
Async XLA Ops:
  7.2 103.5 %copy-start = (bf16[3,1024,256]{2,1,0:T(8,128)(2,1)S(1)}, bf16[3,1024,256]{2,1,0:T(8,128)(2,1)}, u32[]{:S(2)}) copy-start(bf16[3,1024,256]{2,1,0:T(8,128)(2,1)} %param.19) | copy-start | bytes 4718596
  7.2 40.1 %copy-start.7 = (bf16[256]{0:T(256)(128)(2,1)S(1)}, bf16[256]{0:T(256)(128)(2,1)}, u32[]{:S(2)}) copy-start(bf16[256]{0:T(256)(128)(2,1)} %param.23) | copy-start | bytes 1540
  11.6 29.9 %all-to-all-start = ((bf16[128,5,2]{1,2,0:T(2,128)(2,1)}), bf16[128,5,2]{1,2,0:T(2,128)(2,1)S(1)}, u32[]{:S(2)}, u32[]{:S(2)}) async-start(bf16[128,5,2]{1,2,0:T(2,128)(2,1)} %copy.46), calls=%async_computation | async-start | bytes 131072 | tf_op jit(solution)/shard_map/all_to_all | solution.py:71
  41.5 25.3 %all-to-all-start.1 = ((bf16[128,5,256]{2,1,0:T(8,128)(2,1)}), bf16[128,5,256]{2,1,0:T(8,128)(2,1)S(1)}, u32[]{:S(2)}, u32[]{:S(2)}) async-start(bf16[128,5,256]{2,1,0:T(8,128)(2,1)} %all_to_all.30), calls=%async_computation.1 | async-start | bytes 1048576 | tf_op jit(solution)/shard_map/all_to_all | solution.py:70
  47.2 63.4 %all-gather.3.cloned.1.call-start = ((), (), s32[]{:S(2)}) async-start(), calls=%async_computation.6 | async-start | bytes 1966080 | tf_op jit(solution)/shard_map/all_gather | solution.py:85
  47.4 35.0 %copy-start.2 = (s32[256]{0:T(256)S(1)}, s32[256]{0:T(256)}, u32[]{:S(2)}) copy-start(s32[256]{0:T(256)} %param.18) | copy-start | bytes 3076
  47.4 35.0 %copy-start.3 = (s32[256]{0:T(256)S(1)}, s32[256]{0:T(256)}, u32[]{:S(2)}) copy-start(s32[256]{0:T(256)} %param.17) | copy-start | bytes 3076
  82.4 93.7 %reduce-scatter.3.cloned.1.call-start = ((), (), s32[]{:S(2)}) async-start(), calls=%async_computation.7 | async-start | bytes 1966080 | tf_op jit(solution)/shard_map/reduce_scatter | solution.py:119
  116.3 24.9 %copy-start.1 = (bf16[256,1024]{1,0:T(8,128)(2,1)S(1)}, bf16[256,1024]{1,0:T(8,128)(2,1)}, u32[]{:S(2)}) copy-start(bf16[256,1024]{1,0:T(8,128)(2,1)} %param.20) | copy-start | bytes 1572868
  141.2 2.9 copy-start.8
  144.0 78.6 %copy-start.6 = (bf16[512,1024]{1,0:T(8,128)(2,1)S(1)}, bf16[512,1024]{1,0:T(8,128)(2,1)}, u32[]{:S(2)}) copy-start(bf16[512,1024]{1,0:T(8,128)(2,1)} %param.22) | copy-start | bytes 3145732
  144.0 78.6 %all-gather.5.cloned.1.call-start = ((), (), s32[]{:S(2)}) async-start(), calls=%async_computation.8 | async-start | bytes 1966080 | tf_op jit(solution)/shard_map/all_gather | solution.py:126
  185.9 76.6 %reduce-scatter.5.cloned.1.call-start = ((), (), s32[]{:S(2)}) async-start(), calls=%async_computation.9 | async-start | bytes 1966080 | tf_op jit(solution)/shard_map/reduce_scatter | solution.py:132
  230.4 0.7 copy-start.4
  230.4 0.7 copy-start.5
  264.8 34.7 %all-to-all-start.3 = ((bf16[128,5,256]{2,1,0:T(8,128)(2,1)}), bf16[128,5,256]{2,1,0:T(8,128)(2,1)S(1)}, u32[]{:S(2)}, u32[]{:S(2)}) async-start(bf16[128,5,256]{2,1,0:T(8,128)(2,1)} %broadcast_select_fusion), calls=%async_computation.5 | async-start | bytes 1048576 | tf_op jit(solution)/shard_map/all_to_all | solution.py:148
  299.6 26.8 %all-to-all-start.2 = ((bf16[128,5,256]{2,1,0:T(8,128)(2,1)}), bf16[128,5,256]{2,1,0:T(8,128)(2,1)S(1)}, u32[]{:S(2)}, u32[]{:S(2)}) async-start(bf16[128,5,256]{2,1,0:T(8,128)(2,1)} %all_to_all.33), calls=%async_computation.4 | async-start | bytes 1048576 | tf_op jit(solution)/shard_map/all_to_all | solution.py:147
Sparse Core Ops, SparseCore 0:
  82.5 28.0 all-gather.2
  144.1 31.9 reduce-scatter.2
  186.0 36.4 all-gather.4
  230.5 31.9 reduce-scatter.4
where the time goes:
time: 336 us; the launch traced here: 335 us
  waiting for transfers between devices  180 us (54%)
  starting transfers between devices  46.8 us (14%)
  local copies, waits for them, and re-layouts  34.9 us (10%)
  matrix products  33.3 us (10%)
  blocking collectives  16 us (5%)
  between operations  14.8 us (4%)
  other arithmetic  9.16 us (3%)
    all_gather x1, waiting for transfers between devices, on_device(): lax.all_gather(normed_second, 'tp', axis=1, tiled=True)  36.6 us
    reduce_scatter x1, waiting for transfers between devices, on_device(): lax.psum_scatter(attn_terms.astype(jnp.bfloat16), 'tp', scatter_dimension...  32 us
    reduce_scatter x1, waiting for transfers between devices, on_device(): lax.psum_scatter(down_terms.astype(jnp.bfloat16), 'tp', scatter_dimension...  28.2 us
    all_gather x1, waiting for transfers between devices, on_device(): lax.all_gather(normed, 'tp', axis=1, tiled=True)  22 us
    all_to_all x1, waiting for transfers between devices, on_device(): lax.all_to_all(outbox, 'flow', split_axis=0, concat_axis=0, tiled=True)  19 us
    all_to_all x1, starting transfers between devices, on_device(): lax.all_to_all(outcodes, 'flow', split_axis=0, concat_axis=0, tiled=True)  18.4 us
    all_to_all x1, waiting for transfers between devices, on_device(): lax.all_to_all(reply, 'flow', split_axis=0, concat_axis=0, tiled=True)  17.6 us
    psum x2, blocking collectives, normalize(): lax.psum((jnp.sum(values, axis=1, keepdims=True), jnp.sum(values * values...  16 us
  transfers between devices with their start and end apart: 8, of which 8 were waited for; matrix products, arithmetic and copies ran while one was open for 5% of the time, Pallas kernels for 0%

commit v1 on v0

v1 whole, which is shorter than its diff:
```python
import functools

import jax
import jax.numpy as jnp
from jax import lax
from jax.experimental import pallas as pl
from jax.experimental.pallas import tpu as pltpu
from jax.sharding import PartitionSpec as P

MESH = pl.DeviceIdType.MESH
F32, BF16 = jnp.float32, jnp.bfloat16
D = 1024
BLOCK = 128
SLOTS = 768
HEAD_DIM = 64
EPS = 1e-05
DIGIT = 128
LOG2E = 1.4426950408889634
FAR = 1e30
VMEM_LIMIT = 48 * 1024 * 1024
VMEM = pl.BlockSpec(memory_space=pltpu.VMEM)
SMEM = pl.BlockSpec(memory_space=pltpu.SMEM)


def iota(shape, dim):
    return lax.broadcasted_iota(jnp.int32, shape, dim)


def to_row(column):
    n = column.shape[0]
    eye = iota((n, n), 0) == iota((n, n), 1)
    return jnp.sum(jnp.where(eye, column, 0.0), axis=0, keepdims=True)


def to_column(row):
    n = row.shape[1]
    eye = iota((n, n), 0) == iota((n, n), 1)
    return jnp.sum(jnp.where(eye, row, 0.0), axis=1, keepdims=True)


def onehot(mask):
    return jnp.where(mask, 1.0, 0.0).astype(BF16)


def to_blocks(left, right):
    n = left.shape[0] // 8
    return jnp.concatenate([left.reshape(n, 8, 128), right.reshape(n, 8, 128)], axis=1).astype(BF16)


def from_blocks(blocks):
    n = blocks.shape[0]
    wide = blocks.astype(F32)
    return wide[:, :8].reshape(n * 8, 128).astype(BF16), wide[:, 8:].reshape(n * 8, 128).astype(BF16)


def pack_kernel(side, scal_ref, pk_ref, flow_ref, pos_ref, holder_ref, first_ref, out_ref, rows_ref):
    core, place = scal_ref[0], scal_ref[1]
    here, flows = pk_ref.shape[0], holder_ref.shape[1]
    rows = out_ref.shape[0] * 8
    flow = to_column(flow_ref[...].astype(F32)).astype(jnp.int32)
    pos = to_column(pos_ref[...].astype(F32))
    pick = flow == iota((here, flows), 1)
    dest = jnp.sum(jnp.where(pick, holder_ref[...].astype(F32), 0.0), axis=1, keepdims=True)
    first = jnp.sum(jnp.where(pick, first_ref[...].astype(F32), 0.0), axis=1, keepdims=True)
    code = first * BLOCK + pos + 1.0
    high = jnp.floor(code * (1.0 / DIGIT))
    low = code - high * DIGIT
    before = (dest == to_row(dest)) & (iota((here, here), 0) > iota((here, here), 1))
    rank = jnp.sum(jnp.where(before, 1.0, 0.0), axis=1, keepdims=True)
    owner = dest.astype(jnp.int32)
    chip = lax.shift_right_logical(owner, 1)
    major = lax.div(chip, side)
    minor = chip - major * side
    swap = core == 1
    block = 2 * (side * jnp.where(swap, minor, major) + jnp.where(swap, major, minor)) + (owner & 1)
    base = (block * 8).astype(F32)
    base_row = to_row(base)
    rank_row = to_row(rank)
    sub = iota((rows, here), 0).astype(F32)
    take = onehot(sub == base_row + rank_row)
    take_high = onehot(sub == base_row + 5.0)
    take_low = onehot(sub == base_row + 6.0)
    lane = iota((here, 128), 1).astype(F32) - ((place & 15) * 8).astype(F32)
    mine = lane == rank
    left = (
        jnp.dot(take, pk_ref[:, :128], preferred_element_type=F32)
        + jnp.dot(take_high, jnp.where(mine, high, 0.0).astype(BF16), preferred_element_type=F32)
        + jnp.dot(take_low, jnp.where(mine, low, 0.0).astype(BF16), preferred_element_type=F32)
    )
    right = jnp.dot(take, pk_ref[:, 128:], preferred_element_type=F32)
    out_ref[...] = to_blocks(left, right)
    at = iota((here, 128), 1)
    pool = base + 5.0 + jnp.where(first > 0.0, 1.0, 0.0)
    rows_ref[...] = jnp.where(at == 0, base + rank, pool)


def unpack_kernel(in_ref, gain_ref, out_ref, code_ref, fill_ref):
    blocks = in_ref.shape[0]
    rows = blocks * 8
    groups = rows // 128
    left, right = from_blocks(in_ref[...])
    r, g = iota((8, rows), 1), iota((8, rows), 0)
    group = lax.shift_right_logical(r, 7) == g
    high = jnp.dot(onehot(group & ((r & 7) == 5)), left, preferred_element_type=F32)
    low = jnp.dot(onehot(group & ((r & 7) == 6)), left, preferred_element_type=F32)
    code = high * DIGIT + low - 1.0
    code_ref[...] = code
    slot = iota((SLOTS, 128), 0).astype(F32)
    place = jnp.concatenate([onehot(slot == code[i : i + 1]) for i in range(groups)], axis=1)
    out_ref[:SLOTS, :128] = jnp.dot(place, left, preferred_element_type=F32).astype(BF16)
    out_ref[:SLOTS, 128:] = jnp.dot(place, right, preferred_element_type=F32).astype(BF16)
    out_ref[SLOTS:, :] = gain_ref[...]
    fill_ref[...] = lax.dot_general(
        jnp.ones((8, rows), BF16), place, (((1,), (1,)), ((), ())), preferred_element_type=F32
    )


def norm_parts(parts, gains):
    total = sum(jnp.sum(p, axis=1, keepdims=True) for p in parts)
    square = sum(jnp.sum(p * p, axis=1, keepdims=True) for p in parts)
    mean = total / D
    scale = lax.rsqrt(square / D - mean * mean + EPS)
    return [((p - mean) * scale * g).astype(BF16) for p, g in zip(parts, gains)]


def attend_kernel(scal_ref, slope_ref, all_ref, fill_ref, w_ref, out_ref, normed_ref, qkv_ref, far_ref):
    steps = SLOTS // BLOCK
    parts = all_ref.shape[0]
    gains = [all_ref[p, SLOTS : SLOTS + 16, :].astype(F32)[0:1] for p in range(parts)]
    width = out_ref.shape[1]
    edge = scal_ref[2] * BLOCK

    @pl.loop(0, steps)
    def _(step):
        rows = pl.ds(pl.multiple_of(step * BLOCK, BLOCK), BLOCK)
        normed = norm_parts([all_ref[p, rows, :].astype(F32) for p in range(parts)], gains)
        for p in range(parts):
            normed_ref[rows, p * width : (p + 1) * width] = normed[p]
        here = iota((BLOCK, SLOTS), 0) + step * BLOCK
        there = iota((BLOCK, SLOTS), 1)
        allowed = (((here >= edge) == (there >= edge)) & (fill_ref[0:1, :] > 0.0)) | (here == there)
        far_ref[rows, :] = jnp.where(allowed, jnp.abs(here - there).astype(F32) * LOG2E, FAR)

    for k in range(3):
        qkv_ref[k] = jnp.dot(normed_ref[...], w_ref[k], preferred_element_type=F32).astype(BF16)

    @pl.loop(0, steps)
    def _(step):
        rows = pl.ds(pl.multiple_of(step * BLOCK, BLOCK), BLOCK)
        far = far_ref[rows, :]
        first = iota((BLOCK, 128), 1) < HEAD_DIM
        for pair in range(width // 128):
            cols = slice(pair * 128, (pair + 1) * 128)
            query = qkv_ref[0, rows, cols]
            keys, values = qkv_ref[1, :, cols], qkv_ref[2, :, cols]
            halves = []
            for half in range(2):
                mine = jnp.where(first == (half == 0), query, jnp.zeros_like(query))
                scores = lax.dot_general(mine, keys, (((1,), (1,)), ((), ())), preferred_element_type=F32)
                weights = jnp.exp2(
                    scores * (HEAD_DIM**-0.5 * LOG2E) - slope_ref[2 * pair + half] * far
                )
                probs = weights * (1.0 / jnp.sum(weights, axis=1, keepdims=True))
                halves.append(jnp.dot(probs.astype(BF16), values, preferred_element_type=F32))
            out_ref[rows, cols] = jnp.where(first, halves[0], halves[1]).astype(BF16)


def mlp_kernel(scal_ref, att_ref, wo_ref, all_ref, up_ref, down_ref, mid_ref, out_ref, keep_ref):
    parts, width = att_ref.shape[0], att_ref.shape[2]
    gains = [all_ref[p, SLOTS : SLOTS + 16, :].astype(F32)[1:2] for p in range(parts)]
    tall = 256

    @pl.loop(0, SLOTS // tall)
    def _(step):
        rows = pl.ds(pl.multiple_of(step * tall, tall), tall)
        attn = sum(
            jnp.dot(att_ref[p, rows, :], wo_ref[p], preferred_element_type=F32).astype(BF16).astype(F32)
            for p in range(parts)
        )
        middle = [
            (all_ref[p, rows, :].astype(F32) + attn[:, p * width : (p + 1) * width]).astype(BF16)
            for p in range(parts)
        ]
        for p in range(parts):
            keep_ref[p, rows, :] = middle[p]
        normed = jnp.concatenate(norm_parts([m.astype(F32) for m in middle], gains), axis=1)
        upward = jnp.dot(normed, up_ref[...], preferred_element_type=F32)
        active = (0.5 * upward * (1.0 + lax.erf(upward * (0.5**0.5)))).astype(BF16)
        for p in range(parts):
            out_ref[p, rows, :] = jnp.dot(
                active, down_ref[:, p * width : (p + 1) * width], preferred_element_type=F32
            ).astype(BF16)

    mid_ref[...] = keep_ref[scal_ref[3]]


def reply_kernel(scal_ref, enc_ref, code_ref, fill_ref, out_ref):
    rows = out_ref.shape[0] * 8
    edge = scal_ref[2] * BLOCK
    encoded = enc_ref[...]
    slot = iota((128, SLOTS), 1).astype(F32)
    taken = jnp.concatenate(
        [
            jnp.dot(onehot(to_column(code_ref[i : i + 1, :]) == slot), encoded, preferred_element_type=F32)
            for i in range(rows // 128)
        ],
        axis=0,
    )
    second = iota((8, SLOTS), 1) >= edge
    members = jnp.where((fill_ref[...] > 0.0) & (second == (iota((8, SLOTS), 0) == 1)), 1.0, 0.0)
    counts = jnp.sum(members, axis=1, keepdims=True)
    pooled = jnp.dot(members.astype(BF16), encoded, preferred_element_type=F32) / counts
    width = encoded.shape[1]
    sub = iota((rows, width), 0) & 7
    full = jnp.where(sub == 5, pooled[0:1], jnp.where(sub == 6, pooled[1:2], taken))
    out_ref[...] = to_blocks(full[:, :128], full[:, 128:])


def final_kernel(in_ref, rows_ref, enc_ref, ctx_ref):
    left, right = from_blocks(in_ref[...])
    here, rows = rows_ref.shape[0], left.shape[0]
    at = iota((here, rows), 1).astype(F32)
    for column, out in ((0, enc_ref), (1, ctx_ref)):
        pick = onehot(at == rows_ref[:, column : column + 1])
        out[:, :128] = jnp.dot(pick, left, preferred_element_type=F32).astype(BF16)
        out[:, 128:] = jnp.dot(pick, right, preferred_element_type=F32).astype(BF16)


class Spot:
    def __init__(self, side):
        self.side = side
        flow = lax.axis_index("flow")
        self.tp = lax.axis_index("tp")
        self.core = lax.rem(flow, 2)
        chip = flow // 2
        self.y = chip // side
        self.z = lax.rem(chip, side)

    def seen(self, core):
        first = core == 0
        return jnp.where(first, self.y, self.z), jnp.where(first, self.z, self.y)

    def device(self, core, a, b, target_core):
        first = core == 0
        y, z = jnp.where(first, a, b), jnp.where(first, b, a)
        return ((y * self.side + z) * 2 + target_core, self.tp)

    def beside(self, step):
        parts = lax.axis_size("tp")
        return (lax.axis_index("flow"), lax.rem(self.tp + step + parts, parts))


def enter(devices, count):
    barrier = pltpu.get_barrier_semaphore()
    for device in devices:
        pl.semaphore_signal(barrier, inc=1, device_id=device, device_id_type=MESH)
    pl.semaphore_wait(barrier, count)


def remote(src, dst, send, recv, device):
    return pltpu.make_async_remote_copy(
        src_ref=src, dst_ref=dst, send_sem=send, recv_sem=recv, device_id=device, device_id_type=MESH
    )


class Ring:
    def __init__(self, spot, src, out, send, recv, cut):
        self.me = spot.tp
        self.right, self.left = spot.beside(1), spot.beside(-1)
        self.src, self.out, self.send, self.recv = src, out, send, recv
        rows = src.shape[0]
        self.upper, self.lower = pl.ds(0, cut), pl.ds(cut, rows - cut)
        parts = lax.axis_size("tp")
        self.before = lax.rem(self.me + parts - 1, parts)
        self.after = lax.rem(self.me + 1, parts)
        self.far = lax.rem(self.me + 2, parts)

    def copy(self, i, block, part, device, own=False):
        src = self.src.at[part] if own else self.out.at[block, part]
        return remote(src, self.out.at[block, part], self.send.at[i], self.recv.at[i], device)

    def start(self):
        self.first = [
            self.copy(0, self.me, self.upper, self.right, True),
            self.copy(1, self.me, self.lower, self.left, True),
            self.copy(2, self.me, self.lower, self.right, True),
            self.copy(3, self.me, self.upper, self.left, True),
        ]
        for copy in self.first:
            copy.start()

    def forward(self):
        self.copy(0, self.before, self.upper, self.right).wait_recv()
        self.up = self.copy(4, self.before, self.upper, self.right)
        self.up.start()
        self.copy(1, self.after, self.lower, self.left).wait_recv()
        self.down = self.copy(5, self.after, self.lower, self.left)
        self.down.start()

    def finish(self):
        self.copy(2, self.before, self.lower, self.right).wait_recv()
        self.copy(3, self.after, self.upper, self.left).wait_recv()
        self.copy(4, self.far, self.upper, self.right).wait_recv()
        self.copy(5, self.far, self.lower, self.left).wait_recv()
        for copy in (*self.first, self.up, self.down):
            copy.wait_send()


def send_kernel(side, in_ref, w_ref, out_ref, wall_ref, mid, s1, r1, s2, r2, s3, r3):
    spot = Spot(side)
    core = spot.core
    a, b = spot.seen(core)
    other = 1 - core
    oa, ob = spot.seen(other)

    def turn(value, i):
        return lax.rem(value + i, side)

    sources = [spot.device(core, turn(a, i), b, core) for i in range(1, side)]
    sources += [spot.device(core, a, turn(b, i), core) for i in range(1, side)]
    sources += [spot.device(other, oa, turn(ob, i), other) for i in range(side)]
    sources += [spot.beside(1), spot.beside(-1)]
    enter(sources, len(sources))

    first = []
    for i in range(1, side):
        to = turn(a, i)
        copy = remote(in_ref.at[to], mid.at[a], s1.at[i], r1.at[i], spot.device(core, to, b, core))
        copy.start()
        first.append(copy)
    ring = Ring(spot, w_ref, wall_ref, s3, r3, w_ref.shape[0] // 2)
    ring.start()
    mid[a] = in_ref[a]
    wall_ref[spot.tp] = w_ref[...]
    for i in range(1, side):
        came = turn(a, side - i)
        remote(in_ref.at[came], mid.at[came], s1.at[i], r1.at[i], spot.device(core, a, b, other)).wait_recv()
    second = []
    for i in range(side):
        to = turn(b, i)
        for t in range(2):
            target = lax.rem(core + t, 2)
            if i == 0 and t == 0:
                continue
            copy = remote(
                mid.at[:, to, target], out_ref.at[core, b], s2.at[i, t], r2.at[i, t], spot.device(core, a, to, target)
            )
            copy.start()
            second.append(copy)
    out_ref[core, b] = mid[:, b, core]
    ring.forward()
    for i in range(side):
        for t in range(2):
            if i == 0 and t == 0:
                continue
            source = core if t == 0 else other
            came = turn(b if t == 0 else ob, side - i)
            remote(
                mid.at[:, 0, 0], out_ref.at[source, came], s2.at[i, t], r2.at[i, t], spot.device(core, a, b, other)
            ).wait_recv()
    ring.finish()
    for copy in first + second:
        copy.wait_send()


def return_kernel(side, in_ref, out_ref, mid, s1, r1, s2, r2):
    spot = Spot(side)
    core = spot.core
    a, b = spot.seen(core)
    other = 1 - core
    oa, ob = spot.seen(other)

    def turn(value, i):
        return lax.rem(value + i, side)

    sources = [spot.device(core, turn(a, i), b, core) for i in range(1, side)]
    sources += [
        spot.device(core, a, turn(b, i), lax.rem(core + t, 2)) for i in range(side) for t in range(2) if i or t
    ]
    enter(sources, len(sources))

    first = []
    for i in range(side):
        for t in range(2):
            if i == 0 and t == 0:
                continue
            frame, fa, fb = (core, a, b) if t == 0 else (other, oa, ob)
            to = turn(fb, i)
            copy = remote(
                in_ref.at[frame, to], mid.at[:, fb, core], s1.at[i, t], r1.at[i, t], spot.device(frame, fa, to, frame)
            )
            copy.start()
            first.append(copy)
    mid[:, b, core] = in_ref[core, b]
    for i in range(side):
        for t in range(2):
            if i == 0 and t == 0:
                continue
            came = turn(b, side - i)
            remote(
                in_ref.at[0, 0], mid.at[:, came, lax.rem(core + t, 2)], s1.at[i, t], r1.at[i, t],
                spot.device(core, a, b, other),
            ).wait_recv()
    second = []
    for i in range(1, side):
        to = turn(a, i)
        copy = remote(mid.at[to], out_ref.at[a], s2.at[i], r2.at[i], spot.device(core, to, b, core))
        copy.start()
        second.append(copy)
    out_ref[a] = mid[a]
    for i in range(1, side):
        came = turn(a, side - i)
        remote(mid.at[came], out_ref.at[came], s2.at[i], r2.at[i], spot.device(core, a, b, other)).wait_recv()
    for copy in first + second:
        copy.wait_send()


def gather_kernel(cut, in_ref, out_ref, send, recv):
    spot = Spot(1)
    enter([spot.beside(1), spot.beside(-1)], 2)
    ring = Ring(spot, in_ref, out_ref, send, recv, cut)
    ring.start()
    out_ref[spot.tp] = in_ref[...]
    ring.forward()
    ring.finish()


def reduce_kernel(in_ref, mid_ref, out_ref, relay, pair, one, send, recv):
    spot = Spot(1)
    parts = lax.axis_size("tp")
    me = spot.tp
    right, left = spot.beside(1), spot.beside(-1)
    after, before, far = (lax.rem(me + i, parts) for i in (1, parts - 1, 2))
    half = out_ref.shape[0] // 2
    upper, lower = pl.ds(0, half), pl.ds(half, half)
    enter([right, left], 2)
    copies = [
        remote(in_ref.at[far, upper], relay.at[0], send.at[0], recv.at[0], right),
        remote(in_ref.at[far, lower], relay.at[1], send.at[1], recv.at[1], left),
        remote(in_ref.at[after, lower], one.at[1], send.at[2], recv.at[2], right),
        remote(in_ref.at[before, upper], one.at[0], send.at[3], recv.at[3], left),
    ]
    for copy in copies:
        copy.start()
    for i, (to, rows, device) in enumerate(((after, upper, right), (before, lower, left))):
        copies[i].wait_recv()
        copies[i].wait_send()
        relay[i] = (relay[i].astype(F32) + in_ref[to, rows, :].astype(F32)).astype(BF16)
        copy = remote(relay.at[i], pair.at[i], send.at[4 + i], recv.at[4 + i], device)
        copy.start()
        copies.append(copy)
    copies[2].wait_recv()
    copies[3].wait_recv()
    for i, rows in ((0, upper), (1, lower)):
        copies[4 + i].wait_recv()
        terms = in_ref[me, rows, :].astype(F32) + pair[i].astype(F32) + one[i].astype(F32)
        out_ref[rows, :] = (mid_ref[rows, :].astype(F32) + terms).astype(BF16)
    for copy in copies[2:]:
        copy.wait_send()


def shape(*dims, dtype=BF16):
    return jax.ShapeDtypeStruct(dims, dtype)


def local(kernel, outs, specs, scratch=()):
    return pl.pallas_call(
        kernel,
        out_shape=outs,
        in_specs=specs,
        out_specs=jax.tree.map(lambda _: VMEM, outs),
        scratch_shapes=list(scratch),
        compiler_params=pltpu.CompilerParams(vmem_limit_bytes=VMEM_LIMIT),
    )


def linked(kernel, outs, inputs, scratch, number):
    return pl.pallas_call(
        kernel,
        out_shape=outs,
        in_specs=[VMEM] * inputs,
        out_specs=jax.tree.map(lambda _: VMEM, outs),
        scratch_shapes=scratch,
        compiler_params=pltpu.CompilerParams(
            vmem_limit_bytes=VMEM_LIMIT, collective_id=number, has_side_effects=True
        ),
    )


def dma(*dims):
    return pltpu.SemaphoreType.DMA(dims)


def on_device(
    packets, packet_flow, packet_pos, flow_holder_rank, flow_first_block,
    w_qkv, w_out, w_up, w_down, gain_first, gain_second, head_slopes,
):
    owners, parts = lax.axis_size("flow"), lax.axis_size("tp")
    side = int(round((owners // 2) ** 0.5))
    here, width = packets.shape
    flow, tp = lax.axis_index("flow"), lax.axis_index("tp")
    core, chip = flow % 2, flow // 2
    y, z = chip // side, chip % side
    place = core * side * side + jnp.where(core == 0, z * side + y, y * side + z)
    second = jnp.max(jnp.where(flow_holder_rank == flow, flow_first_block, 0))
    scal = jnp.stack([core, place, second, tp]).astype(jnp.int32)
    gains = jnp.concatenate([gain_first[None], gain_second[None], jnp.zeros((14, width), BF16)])

    outbox, rows = local(
        functools.partial(pack_kernel, side),
        (shape(owners, 16, 128), shape(here, 128, dtype=F32)),
        [SMEM] + [VMEM] * 5,
    )(scal, packets, packet_flow[None], packet_pos[None], flow_holder_rank[None], flow_first_block[None])

    inbox, w_out_all = linked(
        functools.partial(send_kernel, side),
        (shape(2, side, side, 16, 128), shape(parts, *w_out.shape)),
        2,
        [pltpu.VMEM((side, side, 2, 16, 128), BF16), dma(side), dma(side), dma(side, 2), dma(side, 2), dma(6), dma(6)],
        1,
    )(outbox.reshape(side, side, 2, 16, 128), w_out)

    buffer, codes, filled = local(
        unpack_kernel,
        (shape(SLOTS + 16, width), shape(8, 128, dtype=F32), shape(8, SLOTS, dtype=F32)),
        [VMEM] * 2,
    )(inbox.reshape(owners, 16, 128), gains)

    whole = linked(
        functools.partial(gather_kernel, 400),
        shape(parts, SLOTS + 16, width), 1, [dma(6), dma(6)], 2,
    )(buffer)

    attended = local(
        attend_kernel,
        shape(SLOTS, width),
        [SMEM, SMEM] + [VMEM] * 3,
        [pltpu.VMEM((SLOTS, D), BF16), pltpu.VMEM((3, SLOTS, width), BF16), pltpu.VMEM((SLOTS, SLOTS), F32)],
    )(scal, head_slopes, whole, filled, w_qkv)

    attended_all = linked(
        functools.partial(gather_kernel, 384),
        shape(parts, SLOTS, width), 1, [dma(6), dma(6)], 3,
    )(attended)

    middle, terms = local(
        mlp_kernel,
        (shape(SLOTS, width), shape(parts, SLOTS, width)),
        [SMEM] + [VMEM] * 5,
        [pltpu.VMEM((parts, SLOTS, width), BF16)],
    )(scal, attended_all, w_out_all, whole, w_up, w_down)

    half = pltpu.VMEM((2, SLOTS // 2, width), BF16)
    encoded = linked(reduce_kernel, shape(SLOTS, width), 2, [half, half, half, dma(6), dma(6)], 4)(terms, middle)

    reply = local(reply_kernel, shape(owners, 16, 128), [SMEM] + [VMEM] * 3)(scal, encoded, codes, filled)

    back = linked(
        functools.partial(return_kernel, side),
        shape(side, side, 2, 16, 128),
        1,
        [pltpu.VMEM((side, side, 2, 16, 128), BF16), dma(side, 2), dma(side, 2), dma(side), dma(side)],
        5,
    )(reply.reshape(2, side, side, 16, 128))

    return local(final_kernel, (shape(here, width), shape(here, width)), [VMEM] * 2)(
        back.reshape(owners, 16, 128), rows
    )


def solution(mesh):
    return jax.shard_map(
        on_device,
        mesh=mesh,
        in_specs=(
            P("flow", "tp"),
            P("flow"),
            P("flow"),
            P(),
            P(),
            P(None, None, "tp"),
            P("tp", None),
            P(None, "tp"),
            P("tp", None),
            P("tp"),
            P("tp"),
            P("tp"),
        ),
        out_specs=(P("flow", "tp"), P("flow", "tp")),
        check_vma=False,
    )
```

time: 336 us -> 145 us (0.43)
  waiting for transfers between devices: 180 us -> 0 us
  Pallas kernels: 0 us -> 134 us
  starting transfers between devices: 46.8 us -> 0 us
  matrix products: 33.3 us -> 0 us
  local copies, waits for them, and re-layouts: 34.9 us -> 7.4 us
  blocking collectives: 16 us -> 0 us
  between operations: 14.8 us -> 0.84 us
  other arithmetic: 9.16 us -> 2.13 us
    pallas_call x0 -> x11, Pallas kernels: none -> 134 us  [the longest x1 33.4 us: on_device(): linked(functools.partial(send_kernel, side), (shape(2, side, side, 16, 12...]
    all_to_all x4 -> x0, waiting for transfers between devices: 60.9 us -> none  [the longest x1 19 us: on_device(): lax.all_to_all(outbox, 'flow', split_axis=0, concat_axis=0, tiled=True)]
    reduce_scatter x2 -> x0, waiting for transfers between devices: 60.3 us -> none  [the longest x1 32 us: on_device(): lax.psum_scatter(attn_terms.astype(jnp.bfloat16), 'tp', scatter_dimension...]
    all_gather x2 -> x0, waiting for transfers between devices: 58.6 us -> none  [the longest x1 36.6 us: on_device(): lax.all_gather(normed_second, 'tp', axis=1, tiled=True)]
    all_to_all x4 -> x0, starting transfers between devices: 46.6 us -> none  [the longest x1 18.4 us: on_device(): lax.all_to_all(outcodes, 'flow', split_axis=0, concat_axis=0, tiled=True)]
    dot_general x12 -> x0, matrix products: 33.3 us -> none  [the longest x4 12 us: one_head(): lax.dot_general(query, key_rows, (((1,), (1,)), ((), ())), preferred_elem...]
    psum x2 -> x0, blocking collectives: 16 us -> none  [normalize(): lax.psum((jnp.sum(values, axis=1, keepdims=True), jnp.sum(values * values...]
    scatter x5 -> x0, local copies, waits for them, and re-layouts: 13 us -> none  [the longest x1 5.44 us: on_device(): jnp.zeros((slots + 1, local_width), jnp.bfloat16).at[target].set(inbox)]
  transfers between devices with their start and end apart: 8 -> 0, of which waited for: 8 -> 0; matrix products, arithmetic and copies ran while one was open for 5% -> 0% of each run, Pallas kernels for 0% -> 0%
where the time goes in v1:
time: 145 us
  Pallas kernels  134 us (92%)
  local copies, waits for them, and re-layouts  7.4 us (5%)
  other arithmetic  2.13 us (1%)
    pallas_call x1, Pallas kernels, on_device(): linked(functools.partial(send_kernel, side), (shape(2, side, side, 16, 12...  33.4 us
    pallas_call x1, Pallas kernels, on_device(): linked(functools.partial(return_kernel, side), shape(side, side, 2, 16, 1...  25.4 us
    pallas_call x1, Pallas kernels, on_device(): linked(functools.partial(gather_kernel, 400), shape(parts, SLOTS + 16, wi...  17.5 us
    pallas_call x1, Pallas kernels, on_device(): linked(functools.partial(gather_kernel, 384), shape(parts, SLOTS, width),...  15.8 us
    pallas_call x1, Pallas kernels, on_device(): linked(reduce_kernel, shape(SLOTS, width), 2, [half, half, half, dma(6),...  14.9 us
    pallas_call x1, Pallas kernels, on_device(): local(attend_kernel, shape(SLOTS, width), [SMEM, SMEM] + [VMEM] * 3, [plt...  13.6 us
    pallas_call x1, Pallas kernels, on_device(): local(mlp_kernel, (shape(SLOTS, width), shape(parts, SLOTS, width)), [SME...  7.69 us
    unnamed x24, local copies, waits for them, and re-layouts  6 us

profile of v1, /device:TPU:1, one launch (start us, length us, event | category | flops | bytes accessed | tf_op | source)
XLA Modules:
  0.0 144.6 jit_solution(15445667572191401078)
XLA Ops:
  0.7 1.3 fusion
  2.0 0.7 pad_add_fusion.scal_ref
  2.7 0.1 pad.2.clone
  2.8 0.7 broadcast_in_dim.30
  3.5 0.7 broadcast_in_dim.31
  4.1 0.1 maximum_maximum_fusion.gain_ref
  4.2 0.0 copy-start.6
  4.2 0.9 copy-done.6
  5.1 0.0 copy-start.7
  5.1 0.7 copy-done.7
  5.8 0.0 copy-start.8
  5.8 0.7 copy-done.8
  6.5 0.0 copy-start.9
  6.5 0.7 copy-done.9
  7.2 0.0 copy-start.10
  7.2 0.7 copy-done.10
  7.8 1.6 %shard_map.131 = (bf16[128,16,128]{2,1,0:T(8,128)(2,1)S(1)}, f32[256,128]{1,0:T(8,128)S(1)}) custom-call(s32[4]{0:T(128)S(1)} %pad_add_fusion.scal_ref, bf16[256,256]{1,0:T(8,128)(2,1)S(1)} %copy-done.6, s32[1,256]{1,0:T(1,128)S(1)} %bitcast.18, s32[1,256]{1,0:T(1,128)S(1)} %bitcast.19, s32[1,256]{1,0:T(1,128)S(1)} %bitcast.17, s32[1,256]{1,0:T(1,128)S(1)} %bitcast.16), custom_call_target="tpu_custom_call" | custom-call | tf_op jit(solution)/shard_map/pallas_call | solution.py:509
  9.5 0.0 copy-start.5
  9.5 1.0 copy-done.5
  10.5 0.0 copy-start.2
  10.5 0.0 copy-start.11
  10.5 33.4 %shard_map.132 = (bf16[2,8,8,16,128]{4,3,2,1,0:T(8,128)(2,1)S(1)}, bf16[4,256,1024]{2,1,0:T(8,128)(2,1)S(1)}) custom-call(bf16[8,8,2,16,128]{4,3,2,1,0:T(8,128)(2,1)S(1)} %bitcast.15, bf16[256,1024]{1,0:T(8,128)(2,1)S(1)} %copy-done.5), custom_call_target="tpu_custom_call" | custom-call | tf_op jit(solution)/shard_map/pallas_call | solution.py:515
  43.9 0.0 copy-start.1
  43.9 1.3 copy-done.1
  45.2 1.5 %shard_map.133 = (bf16[784,256]{1,0:T(8,128)(2,1)S(1)}, f32[8,128]{1,0:T(8,128)S(1)}, f32[8,768]{1,0:T(8,128)S(1)}) custom-call(bf16[128,16,128]{2,1,0:T(8,128)(2,1)S(1)} %bitcast.14, bf16[16,256]{1,0:T(8,128)(2,1)S(1)} %maximum_maximum_fusion.gain_ref), custom_call_target="tpu_custom_call" | custom-call | tf_op jit(solution)/shard_map/pallas_call | solution.py:523
  46.7 17.5 %shard_map.134.all_ref = bf16[4,784,256]{2,1,0:T(8,128)(2,1)S(1)} custom-call(bf16[784,256]{1,0:T(8,128)(2,1)S(1)} %get-tuple-element.13.in_ref), custom_call_target="tpu_custom_call" | custom-call | tf_op jit(solution)/shard_map/pallas_call | solution.py:529
  64.2 0.0 copy-done.2
  64.2 0.0 copy-done.11
  64.3 0.0 copy-start
  64.3 0.0 copy-start.4
  64.3 13.6 %shard_map.135.in_ref = bf16[768,256]{1,0:T(8,128)(2,1)S(1)} custom-call(s32[4]{0:T(128)S(1)} %pad_add_fusion.scal_ref, f32[4]{0:T(128)S(1)} %copy-done.11, bf16[4,784,256]{2,1,0:T(8,128)(2,1)S(1)} %shard_map.134.all_ref, f32[8,768]{1,0:T(8,128)S(1)} %get-tuple-element.14.fill_ref, bf16[3,1024,256]{2,1,0:T(8,128)(2,1)S(1)} %copy-done.2), custom_call_target="tpu_custom_call" | custom-call | tf_op jit(solution)/shard_map/pallas_call | solution.py:534
  77.9 0.0 copy-done
  77.9 0.0 copy-start.3
  77.9 15.8 %shard_map.136.att_ref = bf16[4,768,256]{2,1,0:T(8,128)(2,1)S(1)} custom-call(bf16[768,256]{1,0:T(8,128)(2,1)S(1)} %shard_map.135.in_ref), custom_call_target="tpu_custom_call" | custom-call | tf_op jit(solution)/shard_map/pallas_call | solution.py:541
  93.7 0.0 copy-done.4
  93.7 0.0 copy-done.3
  93.7 7.7 %shard_map.137 = (bf16[768,256]{1,0:T(8,128)(2,1)S(1)}, bf16[4,768,256]{2,1,0:T(8,128)(2,1)S(1)}) custom-call(s32[4]{0:T(128)S(1)} %pad_add_fusion.scal_ref, bf16[4,768,256]{2,1,0:T(8,128)(2,1)S(1)} %shard_map.136.att_ref, bf16[4,256,1024]{2,1,0:T(8,128)(2,1)} %copy-done.1, bf16[4,784,256]{2,1,0:T(8,128)(2,1)} %copy-done, bf16[1024,512]{1,0:T(8,128)(2,1)S(1)} %copy-done.3, ...), custom_call_target="tpu_custom_call" | custom-call | tf_op jit(solution)/shard_map/pallas_call | solution.py:546
  101.4 14.9 %shard_map.138.enc_ref = bf16[768,256]{1,0:T(8,128)(2,1)S(1)} custom-call(bf16[4,768,256]{2,1,0:T(8,128)(2,1)S(1)} %get-tuple-element.16.in_ref, bf16[768,256]{1,0:T(8,128)(2,1)S(1)} %get-tuple-element.17.mid_ref), custom_call_target="tpu_custom_call" | custom-call | tf_op jit(solution)/shard_map/pallas_call | solution.py:554
  116.3 1.5 %shard_map.139 = bf16[128,16,128]{2,1,0:T(8,128)(2,1)S(1)} custom-call(s32[4]{0:T(128)S(1)} %pad_add_fusion.scal_ref, bf16[768,256]{1,0:T(8,128)(2,1)S(1)} %shard_map.138.enc_ref, f32[8,128]{1,0:T(8,128)S(1)} %get-tuple-element.18.code_ref, f32[8,768]{1,0:T(8,128)S(1)} %get-tuple-element.14.fill_ref), custom_call_target="tpu_custom_call" | custom-call | tf_op jit(solution)/shard_map/pallas_call | solution.py:556
  117.8 25.4 %shard_map.140 = bf16[8,8,2,16,128]{4,3,2,1,0:T(8,128)(2,1)S(1)} custom-call(bf16[2,8,8,16,128]{4,3,2,1,0:T(8,128)(2,1)S(1)} %bitcast.13), custom_call_target="tpu_custom_call" | custom-call | tf_op jit(solution)/shard_map/pallas_call | solution.py:558
  143.2 1.4 shard_map.141
  (1 shorter events, 0.0 us)
Async XLA Ops:
  4.2 0.9 copy-start.6
  5.1 0.7 copy-start.7
  5.8 0.7 copy-start.8
  6.5 0.7 copy-start.9
  7.2 0.7 copy-start.10
  9.5 1.0 copy-start.5
  10.5 53.7 %copy-start.2 = (bf16[3,1024,256]{2,1,0:T(8,128)(2,1)S(1)}, bf16[3,1024,256]{2,1,0:T(8,128)(2,1)}, u32[]{:S(2)}) copy-start(bf16[3,1024,256]{2,1,0:T(8,128)(2,1)} %w_ref.3) | copy-start | bytes 4718596
  10.5 53.7 %copy-start.11 = (f32[4]{0:T(128)S(1)}, f32[4]{0:T(128)}, u32[]{:S(2)}) copy-start(f32[4]{0:T(128)} %slope_ref.1) | copy-start | bytes 52
  43.9 1.3 copy-start.1
  64.3 13.6 %copy-start = (bf16[4,784,256]{2,1,0:T(8,128)(2,1)}, bf16[4,784,256]{2,1,0:T(8,128)(2,1)S(1)}, u32[]{:S(2)}) copy-start(bf16[4,784,256]{2,1,0:T(8,128)(2,1)S(1)} %shard_map.134.all_ref) | copy-start | bytes 4816900
  64.3 29.4 %copy-start.4 = (bf16[512,1024]{1,0:T(8,128)(2,1)S(1)}, bf16[512,1024]{1,0:T(8,128)(2,1)}, u32[]{:S(2)}) copy-start(bf16[512,1024]{1,0:T(8,128)(2,1)} %down_ref.1) | copy-start | bytes 3145732
  77.9 15.8 %copy-start.3 = (bf16[1024,512]{1,0:T(8,128)(2,1)S(1)}, bf16[1024,512]{1,0:T(8,128)(2,1)}, u32[]{:S(2)}) copy-start(bf16[1024,512]{1,0:T(8,128)(2,1)} %up_ref.1) | copy-start | bytes 3145732

commit v2 on v1

--- a/solution.py
+++ b/solution.py
@@ -17,9 +17,11 @@
 DIGIT = 128
 LOG2E = 1.4426950408889634
 FAR = 1e30
+TALL = 256
 VMEM_LIMIT = 48 * 1024 * 1024
 VMEM = pl.BlockSpec(memory_space=pltpu.VMEM)
 SMEM = pl.BlockSpec(memory_space=pltpu.SMEM)
+HBM = pl.BlockSpec(memory_space=pltpu.HBM)
 
 
 def iota(shape, dim):
@@ -53,15 +55,28 @@
     return wide[:, :8].reshape(n * 8, 128).astype(BF16), wide[:, 8:].reshape(n * 8, 128).astype(BF16)
 
 
-def pack_kernel(side, scal_ref, pk_ref, flow_ref, pos_ref, holder_ref, first_ref, out_ref, rows_ref):
-    core, place = scal_ref[0], scal_ref[1]
-    here, flows = pk_ref.shape[0], holder_ref.shape[1]
+def pack_kernel(side, *refs):
+    sources, (out_ref, rows_ref, edge_ref), holds, sem = refs[:5], refs[5:8], refs[8:13], refs[13]
+    copies = [pltpu.make_async_copy(s, h, sem.at[i]) for i, (s, h) in enumerate(zip(sources, holds))]
+    for copy in copies:
+        copy.start()
+    for copy in copies:
+        copy.wait()
+    pk_ref = holds[0]
+    flow_row, pos_row, holder, first_block = (ref[...].astype(F32)[None] for ref in holds[1:])
+    me = lax.axis_index("flow")
+    core = lax.rem(me, 2)
+    mine_major, mine_minor = lax.div(lax.div(me, 2), side), lax.rem(lax.div(me, 2), side)
+    place = core * side * side + jnp.where(core == 0, mine_minor * side + mine_major, mine_major * side + mine_minor)
+    here, flows = pk_ref.shape[0], holder.shape[1]
     rows = out_ref.shape[0] * 8
-    flow = to_column(flow_ref[...].astype(F32)).astype(jnp.int32)
-    pos = to_column(pos_ref[...].astype(F32))
+    second = jnp.max(jnp.where(holder == me.astype(F32), first_block, 0.0), axis=1, keepdims=True)
+    edge_ref[...] = jnp.broadcast_to(second * BLOCK, edge_ref.shape)
+    flow = to_column(flow_row).astype(jnp.int32)
+    pos = to_column(pos_row)
     pick = flow == iota((here, flows), 1)
-    dest = jnp.sum(jnp.where(pick, holder_ref[...].astype(F32), 0.0), axis=1, keepdims=True)
-    first = jnp.sum(jnp.where(pick, first_ref[...].astype(F32), 0.0), axis=1, keepdims=True)
+    dest = jnp.sum(jnp.where(pick, holder, 0.0), axis=1, keepdims=True)
+    first = jnp.sum(jnp.where(pick, first_block, 0.0), axis=1, keepdims=True)
     code = first * BLOCK + pos + 1.0
     high = jnp.floor(code * (1.0 / DIGIT))
     low = code - high * DIGIT
@@ -94,7 +109,7 @@
     rows_ref[...] = jnp.where(at == 0, base + rank, pool)
 
 
-def unpack_kernel(in_ref, gain_ref, out_ref, code_ref, fill_ref):
+def unpack_kernel(in_ref, gain1_ref, gain2_ref, out_ref, code_ref, fill_ref):
     blocks = in_ref.shape[0]
     rows = blocks * 8
     groups = rows // 128
@@ -109,7 +124,8 @@
     place = jnp.concatenate([onehot(slot == code[i : i + 1]) for i in range(groups)], axis=1)
     out_ref[:SLOTS, :128] = jnp.dot(place, left, preferred_element_type=F32).astype(BF16)
     out_ref[:SLOTS, 128:] = jnp.dot(place, right, preferred_element_type=F32).astype(BF16)
-    out_ref[SLOTS:, :] = gain_ref[...]
+    one, two = gain1_ref[...].astype(F32)[None], gain2_ref[...].astype(F32)[None]
+    out_ref[SLOTS:, :] = jnp.where(iota((16, out_ref.shape[1]), 0) == 0, one, two).astype(BF16)
     fill_ref[...] = lax.dot_general(
         jnp.ones((8, rows), BF16), place, (((1,), (1,)), ((), ())), preferred_element_type=F32
     )
@@ -123,80 +139,9 @@
     return [((p - mean) * scale * g).astype(BF16) for p, g in zip(parts, gains)]
 
 
-def attend_kernel(scal_ref, slope_ref, all_ref, fill_ref, w_ref, out_ref, normed_ref, qkv_ref, far_ref):
-    steps = SLOTS // BLOCK
-    parts = all_ref.shape[0]
-    gains = [all_ref[p, SLOTS : SLOTS + 16, :].astype(F32)[0:1] for p in range(parts)]
-    width = out_ref.shape[1]
-    edge = scal_ref[2] * BLOCK
-
-    @pl.loop(0, steps)
-    def _(step):
-        rows = pl.ds(pl.multiple_of(step * BLOCK, BLOCK), BLOCK)
-        normed = norm_parts([all_ref[p, rows, :].astype(F32) for p in range(parts)], gains)
-        for p in range(parts):
-            normed_ref[rows, p * width : (p + 1) * width] = normed[p]
-        here = iota((BLOCK, SLOTS), 0) + step * BLOCK
-        there = iota((BLOCK, SLOTS), 1)
-        allowed = (((here >= edge) == (there >= edge)) & (fill_ref[0:1, :] > 0.0)) | (here == there)
-        far_ref[rows, :] = jnp.where(allowed, jnp.abs(here - there).astype(F32) * LOG2E, FAR)
-
-    for k in range(3):
-        qkv_ref[k] = jnp.dot(normed_ref[...], w_ref[k], preferred_element_type=F32).astype(BF16)
-
-    @pl.loop(0, steps)
-    def _(step):
-        rows = pl.ds(pl.multiple_of(step * BLOCK, BLOCK), BLOCK)
-        far = far_ref[rows, :]
-        first = iota((BLOCK, 128), 1) < HEAD_DIM
-        for pair in range(width // 128):
-            cols = slice(pair * 128, (pair + 1) * 128)
-            query = qkv_ref[0, rows, cols]
-            keys, values = qkv_ref[1, :, cols], qkv_ref[2, :, cols]
-            halves = []
-            for half in range(2):
-                mine = jnp.where(first == (half == 0), query, jnp.zeros_like(query))
-                scores = lax.dot_general(mine, keys, (((1,), (1,)), ((), ())), preferred_element_type=F32)
-                weights = jnp.exp2(
-                    scores * (HEAD_DIM**-0.5 * LOG2E) - slope_ref[2 * pair + half] * far
-                )
-                probs = weights * (1.0 / jnp.sum(weights, axis=1, keepdims=True))
-                halves.append(jnp.dot(probs.astype(BF16), values, preferred_element_type=F32))
-            out_ref[rows, cols] = jnp.where(first, halves[0], halves[1]).astype(BF16)
-
-
-def mlp_kernel(scal_ref, att_ref, wo_ref, all_ref, up_ref, down_ref, mid_ref, out_ref, keep_ref):
-    parts, width = att_ref.shape[0], att_ref.shape[2]
-    gains = [all_ref[p, SLOTS : SLOTS + 16, :].astype(F32)[1:2] for p in range(parts)]
-    tall = 256
-
-    @pl.loop(0, SLOTS // tall)
-    def _(step):
-        rows = pl.ds(pl.multiple_of(step * tall, tall), tall)
-        attn = sum(
-            jnp.dot(att_ref[p, rows, :], wo_ref[p], preferred_element_type=F32).astype(BF16).astype(F32)
-            for p in range(parts)
-        )
-        middle = [
-            (all_ref[p, rows, :].astype(F32) + attn[:, p * width : (p + 1) * width]).astype(BF16)
-            for p in range(parts)
-        ]
-        for p in range(parts):
-            keep_ref[p, rows, :] = middle[p]
-        normed = jnp.concatenate(norm_parts([m.astype(F32) for m in middle], gains), axis=1)
-        upward = jnp.dot(normed, up_ref[...], preferred_element_type=F32)
-        active = (0.5 * upward * (1.0 + lax.erf(upward * (0.5**0.5)))).astype(BF16)
-        for p in range(parts):
-            out_ref[p, rows, :] = jnp.dot(
-                active, down_ref[:, p * width : (p + 1) * width], preferred_element_type=F32
-            ).astype(BF16)
-
-    mid_ref[...] = keep_ref[scal_ref[3]]
-
-
-def reply_kernel(scal_ref, enc_ref, code_ref, fill_ref, out_ref):
+def reply_kernel(edge_ref, enc_ref, code_ref, fill_ref, out_ref):
     rows = out_ref.shape[0] * 8
-    edge = scal_ref[2] * BLOCK
+    edge = edge_ref[0:1, 0:1]
     encoded = enc_ref[...]
     slot = iota((128, SLOTS), 1).astype(F32)
     taken = jnp.concatenate(
@@ -206,7 +151,7 @@
         ],
         axis=0,
     )
-    second = iota((8, SLOTS), 1) >= edge
+    second = iota((8, SLOTS), 1).astype(F32) >= edge
     members = jnp.where((fill_ref[...] > 0.0) & (second == (iota((8, SLOTS), 0) == 1)), 1.0, 0.0)
     counts = jnp.sum(members, axis=1, keepdims=True)
     pooled = jnp.dot(members.astype(BF16), encoded, preferred_element_type=F32) / counts
@@ -264,19 +209,19 @@
 
 
 class Ring:
-    def __init__(self, spot, src, out, send, recv, cut):
+    def __init__(self, spot, src, out, send, recv, cut, start=0, rows=None):
         self.me = spot.tp
         self.right, self.left = spot.beside(1), spot.beside(-1)
         self.src, self.out, self.send, self.recv = src, out, send, recv
-        rows = src.shape[0]
-        self.upper, self.lower = pl.ds(0, cut), pl.ds(cut, rows - cut)
+        rows = src.shape[0] if rows is None else rows
+        self.upper, self.lower = pl.ds(start, cut), pl.ds(start + cut, rows - cut)
         parts = lax.axis_size("tp")
         self.before = lax.rem(self.me + parts - 1, parts)
         self.after = lax.rem(self.me + 1, parts)
         self.far = lax.rem(self.me + 2, parts)
 
     def copy(self, i, block, part, device, own=False):
-        src = self.src.at[part] if own else self.out.at[block, part]
+        src = self.src.at[part] if own and self.src is not None else self.out.at[block, part]
         return remote(src, self.out.at[block, part], self.send.at[i], self.recv.at[i], device)
 
     def start(self):
@@ -425,38 +370,151 @@
     ring.finish()
 
 
-def reduce_kernel(in_ref, mid_ref, out_ref, relay, pair, one, send, recv):
+class Sum:
+    def __init__(self, spot, terms, relay, pair, one, send, recv, start, rows):
+        parts = lax.axis_size("tp")
+        self.me = spot.tp
+        self.right, self.left = spot.beside(1), spot.beside(-1)
+        self.after, self.before, self.far = (lax.rem(self.me + i, parts) for i in (1, parts - 1, 2))
+        self.terms, self.relay, self.pair, self.one = terms, relay, pair, one
+        self.send, self.recv = send, recv
+        self.upper, self.lower = pl.ds(start, rows // 2), pl.ds(start + rows // 2, rows // 2)
+
+    def copy(self, i, src, dst, device):
+        copy = remote(src, dst, self.send.at[i], self.recv.at[i], device)
+        copy.start()
+        return copy
+
+    def start(self):
+        terms = self.terms
+        self.copies = [
+            self.copy(0, terms.at[self.far, self.upper], self.relay.at[0], self.right),
+            self.copy(1, terms.at[self.far, self.lower], self.relay.at[1], self.left),
+            self.copy(2, terms.at[self.after, self.lower], self.one.at[1], self.right),
+            self.copy(3, terms.at[self.before, self.upper], self.one.at[0], self.left),
+        ]
+
+    def forward(self):
+        for i, (to, rows, device) in enumerate(
+            ((self.after, self.upper, self.right), (self.before, self.lower, self.left))
+        ):
+            self.copies[i].wait_recv()
+            self.relay[i] = (self.relay[i].astype(F32) + self.terms[to, rows, :].astype(F32)).astype(BF16)
+            self.copies.append(self.copy(4 + i, self.relay.at[i], self.pair.at[i], device))
+
+    def finish(self, keep, out):
+        for i in range(2, 6):
+            self.copies[i].wait_recv()
+        for i, rows in ((0, self.upper), (1, self.lower)):
+            terms = self.terms[self.me, rows, :].astype(F32) + self.pair[i].astype(F32) + self.one[i].astype(F32)
+            out[rows, :] = (keep[self.me, rows, :].astype(F32) + terms).astype(BF16)
+        for copy in self.copies:
+            copy.wait_send()
+
+
+def core_kernel(
+    slope_ref, edge_ref, all_ref, fill_ref, wq_any, wo_any, up_any, down_any, out_ref,
+    normed_ref, qkv_ref, far_ref, att_ref, keep_ref, terms_ref, relay, pair, one,
+    wq_ref, wo_ref, up_ref, down_ref, wsem, gsend, grecv, ssend, srecv,
+):
     spot = Spot(1)
-    parts = lax.axis_size("tp")
+    barrier = pltpu.get_barrier_semaphore()
+    for device in (spot.beside(1), spot.beside(-1)):
+        pl.semaphore_signal(barrier, inc=1, device_id=device, device_id_type=MESH)
+    loads = [
+        pltpu.make_async_copy(src, dst, wsem.at[i])
+        for i, (src, dst) in enumerate(
+            ((wq_any, wq_ref), (wo_any, wo_ref), (up_any, up_ref), (down_any, down_ref))
+        )
+    ]
+    for load in loads:
+        load.start()
+    parts, width = att_ref.shape[0], att_ref.shape[2]
     me = spot.tp
-    right, left = spot.beside(1), spot.beside(-1)
-    after, before, far = (lax.rem(me + i, parts) for i in (1, parts - 1, 2))
-    half = out_ref.shape[0] // 2
-    upper, lower = pl.ds(0, half), pl.ds(half, half)
-    enter([right, left], 2)
-    copies = [
-        remote(in_ref.at[far, upper], relay.at[0], send.at[0], recv.at[0], right),
-        remote(in_ref.at[far, lower], relay.at[1], send.at[1], recv.at[1], left),
-        remote(in_ref.at[after, lower], one.at[1], send.at[2], recv.at[2], right),
-        remote(in_ref.at[before, upper], one.at[0], send.at[3], recv.at[3], left),
+    chunks = SLOTS // TALL
+    gains = [all_ref[p, SLOTS : SLOTS + 16, :].astype(F32) for p in range(parts)]
+    edge = edge_ref[0:1, 0:1]
+
+    @pl.loop(0, SLOTS // BLOCK)
+    def _(step):
+        rows = pl.ds(pl.multiple_of(step * BLOCK, BLOCK), BLOCK)
+        normed = norm_parts([all_ref[p, rows, :].astype(F32) for p in range(parts)], [g[0:1] for g in gains])
+        for p in range(parts):
+            normed_ref[rows, p * width : (p + 1) * width] = normed[p]
+
+    loads[0].wait()
+    for k in range(3):
+        qkv_ref[k] = jnp.dot(normed_ref[...], wq_ref[k], preferred_element_type=F32).astype(BF16)
+
+    def attend(chunk):
+        rows = pl.ds(chunk * TALL, TALL)
+        here = (iota((TALL, SLOTS), 0) + chunk * TALL).astype(F32)
+        there = iota((TALL, SLOTS), 1).astype(F32)
+        allowed = (((here >= edge) == (there >= edge)) & (fill_ref[0:1, :] > 0.0)) | (here == there)
+        far_ref[...] = jnp.where(allowed, jnp.abs(here - there) * LOG2E, FAR)
+        first = iota((TALL, 128), 1) < HEAD_DIM
+        for two in range(width // 128):
+            cols = slice(two * 128, (two + 1) * 128)
+            query = qkv_ref[0, rows, cols]
+            keys, values = qkv_ref[1, :, cols], qkv_ref[2, :, cols]
+            halves = []
+            for half in range(2):
+                mine = jnp.where(first == (half == 0), query, jnp.zeros_like(query))
+                scores = lax.dot_general(mine, keys, (((1,), (1,)), ((), ())), preferred_element_type=F32)
+                weights = jnp.exp2(
+                    scores * (HEAD_DIM**-0.5 * LOG2E) - slope_ref[2 * two + half] * far_ref[...]
+                )
+                probs = weights * (1.0 / jnp.sum(weights, axis=1, keepdims=True))
+                halves.append(jnp.dot(probs.astype(BF16), values, preferred_element_type=F32))
+            att_ref[me, rows, cols] = jnp.where(first, halves[0], halves[1]).astype(BF16)
+
+    def forward_layer(chunk):
+        rows = pl.ds(chunk * TALL, TALL)
+        attn = sum(
+            jnp.dot(att_ref[p, rows, :], wo_ref[p], preferred_element_type=F32).astype(BF16).astype(F32)
+            for p in range(parts)
+        )
+        middle = [
+            (all_ref[p, rows, :].astype(F32) + attn[:, p * width : (p + 1) * width]).astype(BF16)
+            for p in range(parts)
+        ]
+        for p in range(parts):
+            keep_ref[p, rows, :] = middle[p]
+        normed = jnp.concatenate(norm_parts([m.astype(F32) for m in middle], [g[1:2] for g in gains]), axis=1)
+        upward = jnp.dot(normed, up_ref[...], preferred_element_type=F32)
+        active = (0.5 * upward * (1.0 + lax.erf(upward * (0.5**0.5)))).astype(BF16)
+        for p in range(parts):
+            terms_ref[p, rows, :] = jnp.dot(
+                active, down_ref[:, p * width : (p + 1) * width], preferred_element_type=F32
+            ).astype(BF16)
+
+    rings = [
+        Ring(spot, None, att_ref, gsend.at[c], grecv.at[c], TALL // 2, c * TALL, TALL) for c in range(chunks)
     ]
-    for copy in copies:
-        copy.start()
-    for i, (to, rows, device) in enumerate(((after, upper, right), (before, lower, left))):
-        copies[i].wait_recv()
-        copies[i].wait_send()
-        relay[i] = (relay[i].astype(F32) + in_ref[to, rows, :].astype(F32)).astype(BF16)
-        copy = remote(relay.at[i], pair.at[i], send.at[4 + i], recv.at[4 + i], device)
-        copy.start()
-        copies.append(copy)
-    copies[2].wait_recv()
-    copies[3].wait_recv()
-    for i, rows in ((0, upper), (1, lower)):
-        copies[4 + i].wait_recv()
-        terms = in_ref[me, rows, :].astype(F32) + pair[i].astype(F32) + one[i].astype(F32)
-        out_ref[rows, :] = (mid_ref[rows, :].astype(F32) + terms).astype(BF16)
-    for copy in copies[2:]:
-        copy.wait_send()
+    sums = [
+        Sum(spot, terms_ref, relay.at[c], pair.at[c], one.at[c], ssend.at[c], srecv.at[c], c * TALL, TALL)
+        for c in range(chunks)
+    ]
+    for c in range(chunks):
+        attend(c)
+        if c == 0:
+            pl.semaphore_wait(barrier, 2)
+        rings[c].start()
+        if c:
+            rings[c - 1].forward()
+    for load in loads[1:]:
+        load.wait()
+    for c in range(chunks):
+        if c == 1:
+            rings[chunks - 1].forward()
+        rings[c].finish()
+        forward_layer(c)
+        sums[c].start()
+        if c:
+            sums[c - 1].forward()
+    sums[chunks - 1].forward()
+    for c in range(chunks):
+        sums[c].finish(keep_ref, out_ref)
 
 
 def shape(*dims, dtype=BF16):
@@ -478,7 +536,7 @@
     return pl.pallas_call(
         kernel,
         out_shape=outs,
-        in_specs=[VMEM] * inputs,
+        in_specs=[VMEM] * inputs if isinstance(inputs, int) else inputs,
         out_specs=jax.tree.map(lambda _: VMEM, outs),
         scratch_shapes=scratch,
         compiler_params=pltpu.CompilerParams(
@@ -498,19 +556,14 @@
     owners, parts = lax.axis_size("flow"), lax.axis_size("tp")
     side = int(round((owners // 2) ** 0.5))
     here, width = packets.shape
-    flow, tp = lax.axis_index("flow"), lax.axis_index("tp")
-    core, chip = flow % 2, flow // 2
-    y, z = chip // side, chip % side
-    place = core * side * side + jnp.where(core == 0, z * side + y, y * side + z)
-    second = jnp.max(jnp.where(flow_holder_rank == flow, flow_first_block, 0))
-    scal = jnp.stack([core, place, second, tp]).astype(jnp.int32)
-    gains = jnp.concatenate([gain_first[None], gain_second[None], jnp.zeros((14, width), BF16)])
-
-    outbox, rows = local(
+    given = (packets, packet_flow, packet_pos, flow_holder_rank, flow_first_block)
+
+    outbox, rows, edge = local(
         functools.partial(pack_kernel, side),
-        (shape(owners, 16, 128), shape(here, 128, dtype=F32)),
-        [SMEM] + [VMEM] * 5,
-    )(scal, packets, packet_flow[None], packet_pos[None], flow_holder_rank[None], flow_first_block[None])
+        (shape(owners, 16, 128), shape(here, 128, dtype=F32), shape(8, 128, dtype=F32)),
+        [HBM] * 5,
+        [pltpu.VMEM(v.shape, v.dtype) for v in given] + [dma(5)],
+    )(*given)
 
     inbox, w_out_all = linked(
         functools.partial(send_kernel, side),
@@ -523,37 +576,31 @@
     buffer, codes, filled = local(
         unpack_kernel,
         (shape(SLOTS + 16, width), shape(8, 128, dtype=F32), shape(8, SLOTS, dtype=F32)),
-        [VMEM] * 2,
-    )(inbox.reshape(owners, 16, 128), gains)
+        [VMEM] * 3,
+    )(inbox.reshape(owners, 16, 128), gain_first, gain_second)
 
     whole = linked(
         functools.partial(gather_kernel, 400),
         shape(parts, SLOTS + 16, width), 1, [dma(6), dma(6)], 2,
     )(buffer)
 
-    attended = local(
-        attend_kernel,
+    chunks, half = SLOTS // TALL, TALL // 2
+    some = pltpu.VMEM((chunks, 2, half, width), BF16)
+    full = pltpu.VMEM((parts, SLOTS, width), BF16)
+    encoded = linked(
+        core_kernel,
         shape(SLOTS, width),
-        [SMEM, SMEM] + [VMEM] * 3,
-        [pltpu.VMEM((SLOTS, D), BF16), pltpu.VMEM((3, SLOTS, width), BF16), pltpu.VMEM((SLOTS, SLOTS), F32)],
-    )(scal, head_slopes, whole, filled, w_qkv)
-
-    attended_all = linked(
-        functools.partial(gather_kernel, 384),
-        shape(parts, SLOTS, width), 1, [dma(6), dma(6)], 3,
-    )(attended)
-
-    middle, terms = local(
-        mlp_kernel,
-        (shape(SLOTS, width), shape(parts, SLOTS, width)),
-        [SMEM] + [VMEM] * 5,
-        [pltpu.VMEM((parts, SLOTS, width), BF16)],
-    )(scal, attended_all, w_out_all, whole, w_up, w_down)
-
-    half = pltpu.VMEM((2, SLOTS // 2, width), BF16)
-    encoded = linked(reduce_kernel, shape(SLOTS, width), 2, [half, half, half, dma(6), dma(6)], 4)(terms, middle)
-
-    reply = local(reply_kernel, shape(owners, 16, 128), [SMEM] + [VMEM] * 3)(scal, encoded, codes, filled)
+        [SMEM, VMEM, VMEM, VMEM] + [HBM] * 4,
+        [
+            pltpu.VMEM((SLOTS, D), BF16), pltpu.VMEM((3, SLOTS, width), BF16), pltpu.VMEM((TALL, SLOTS), F32),
+            full, full, full, some, some, some,
+            *(pltpu.VMEM(w.shape, BF16) for w in (w_qkv, w_out_all, w_up, w_down)),
+            dma(4), dma(chunks, 6), dma(chunks, 6), dma(chunks, 6), dma(chunks, 6),
+        ],
+        3,
+    )(head_slopes, edge, whole, filled, w_qkv, w_out_all, w_up, w_down)
+
+    reply = local(reply_kernel, shape(owners, 16, 128), [VMEM] * 4)(edge, encoded, codes, filled)
 
     back = linked(
         functools.partial(return_kernel, side),

time: 145 us -> 124 us (0.86)
  Pallas kernels: 134 us -> 116 us
  other arithmetic: 2.13 us -> 0 us
    pallas_call x5 -> x2, Pallas kernels: 53.4 us -> 36.3 us  [the longest x1 35.3 us: on_device(): linked(core_kernel, shape(SLOTS, width), [SMEM, VMEM, VMEM, VMEM] + [HBM]...]
    unnamed x24 -> x26, local copies, waits for them, and re-layouts: 6 us -> 7.3 us
where the time goes in v2:
time: 124 us
  Pallas kernels  116 us (94%)
  local copies, waits for them, and re-layouts  7.3 us (6%)
    pallas_call x1, Pallas kernels, on_device(): linked(core_kernel, shape(SLOTS, width), [SMEM, VMEM, VMEM, VMEM] + [HBM]...  35.3 us
    pallas_call x1, Pallas kernels, on_device(): linked(functools.partial(send_kernel, side), (shape(2, side, side, 16, 12...  33.4 us
    pallas_call x1, Pallas kernels, on_device(): linked(functools.partial(return_kernel, side), shape(side, side, 2, 16, 1...  24.5 us
    pallas_call x1, Pallas kernels, on_device(): linked(functools.partial(gather_kernel, 400), shape(parts, SLOTS + 16, wi...  17.4 us
    unnamed x26, local copies, waits for them, and re-layouts  7.3 us

profile of v2, /device:TPU:1, one launch (start us, length us, event | category | flops | bytes accessed | tf_op | source)
XLA Modules:
  0.0 123.8 jit_solution(12796513369283965472)
XLA Ops:
  0.6 0.0 copy-start.5
  0.6 0.9 copy-done.5
  1.5 0.0 copy-start.6
  1.5 0.7 copy-done.6
  2.2 0.0 copy-start.7
  2.2 0.7 copy-done.7
  2.9 0.0 copy-start.8
  2.9 0.7 copy-done.8
  3.6 0.0 copy-start.9
  3.6 0.7 copy-done.9
  4.3 0.0 copy-start.3
  4.3 1.3 %shard_map.131 = (bf16[128,16,128]{2,1,0:T(8,128)(2,1)S(1)}, f32[256,128]{1,0:T(8,128)S(1)}, f32[8,128]{1,0:T(8,128)S(1)}) custom-call(bf16[256,256]{1,0:T(8,128)(2,1)S(1)} %copy-done.5, s32[256]{0:T(256)S(1)} %copy-done.6, s32[256]{0:T(256)S(1)} %copy-done.7, s32[256]{0:T(256)S(1)} %copy-done.8, s32[256]{0:T(256)S(1)} %copy-done.9), custom_call_target="tpu_custom_call" | custom-call | tf_op jit(solution)/shard_map/pallas_call | solution.py:561
  5.5 0.0 copy-start.4
  5.6 1.0 copy-done.4
  6.6 0.0 copy-start.1
  6.6 0.0 copy-start.2
  6.6 0.0 copy-start.10
  6.6 33.4 %shard_map.132 = (bf16[2,8,8,16,128]{4,3,2,1,0:T(8,128)(2,1)S(1)}, bf16[4,256,1024]{2,1,0:T(8,128)(2,1)S(1)}) custom-call(bf16[8,8,2,16,128]{4,3,2,1,0:T(8,128)(2,1)S(1)} %bitcast.7, bf16[256,1024]{1,0:T(8,128)(2,1)S(1)} %copy-done.4), custom_call_target="tpu_custom_call" | custom-call | tf_op jit(solution)/shard_map/pallas_call | solution.py:568
  40.0 0.0 copy-start
  40.0 1.3 %copy-done = bf16[4,256,1024]{2,1,0:T(8,128)(2,1)} copy-done((bf16[4,256,1024]{2,1,0:T(8,128)(2,1)}, bf16[4,256,1024]{2,1,0:T(8,128)(2,1)S(1)}, u32[]{:S(2)}) %copy-start) | copy-done | bytes 2097176
  41.3 0.0 copy-start.11
  41.3 0.7 copy-done.11
  42.0 0.0 copy-start.12
  42.0 0.7 copy-done.12
  42.6 1.5 %shard_map.133 = (bf16[784,256]{1,0:T(8,128)(2,1)S(1)}, f32[8,128]{1,0:T(8,128)S(1)}, f32[8,768]{1,0:T(8,128)S(1)}) custom-call(bf16[128,16,128]{2,1,0:T(8,128)(2,1)S(1)} %bitcast.6, bf16[256]{0:T(256)(128)(2,1)S(1)} %copy-done.11, bf16[256]{0:T(256)(128)(2,1)S(1)} %copy-done.12), custom_call_target="tpu_custom_call" | custom-call | tf_op jit(solution)/shard_map/pallas_call | solution.py:576
  44.1 17.4 %shard_map.134.all_ref = bf16[4,784,256]{2,1,0:T(8,128)(2,1)S(1)} custom-call(bf16[784,256]{1,0:T(8,128)(2,1)S(1)} %get-tuple-element.13.in_ref), custom_call_target="tpu_custom_call" | custom-call | tf_op jit(solution)/shard_map/pallas_call | solution.py:582
  61.6 0.0 copy-done.3
  61.6 0.0 copy-done.1
  61.6 0.0 copy-done.2
  61.6 0.0 copy-done.10
  61.6 35.3 %shard_map.135.enc_ref = bf16[768,256]{1,0:T(8,128)(2,1)S(1)} custom-call(f32[4]{0:T(128)S(1)} %copy-done.10, f32[8,128]{1,0:T(8,128)S(1)} %get-tuple-element.10.edge_ref, bf16[4,784,256]{2,1,0:T(8,128)(2,1)S(1)} %shard_map.134.all_ref, f32[8,768]{1,0:T(8,128)S(1)} %get-tuple-element.14.fill_ref, bf16[3,1024,256]{2,1,0:T(8,128)(2,1)S(1)} %copy-done.1, ...), custom_call_target="tpu_custom_call" | custom-call | tf_op jit(solution)/shard_map/pallas_call | solution.py:590
  97.0 0.9 shard_map.136
  97.9 24.5 %shard_map.137 = bf16[8,8,2,16,128]{4,3,2,1,0:T(8,128)(2,1)S(1)} custom-call(bf16[2,8,8,16,128]{4,3,2,1,0:T(8,128)(2,1)S(1)} %bitcast.5), custom_call_target="tpu_custom_call" | custom-call | tf_op jit(solution)/shard_map/pallas_call | solution.py:605
  122.4 1.4 %shard_map.138 = (bf16[256,256]{1,0:T(8,128)(2,1)}, bf16[256,256]{1,0:T(8,128)(2,1)}) custom-call(bf16[128,16,128]{2,1,0:T(8,128)(2,1)S(1)} %bitcast.4, f32[256,128]{1,0:T(8,128)S(1)} %get-tuple-element.17.rows_ref), custom_call_target="tpu_custom_call" | custom-call | tf_op jit(solution)/shard_map/pallas_call | solution.py:613
Async XLA Ops:
  0.6 0.9 copy-start.5
  1.5 0.7 copy-start.6
  2.2 0.7 copy-start.7
  2.9 0.7 copy-start.8
  3.6 0.7 copy-start.9
  4.3 57.3 %copy-start.3 = (bf16[512,1024]{1,0:T(8,128)(2,1)S(1)}, bf16[512,1024]{1,0:T(8,128)(2,1)}, u32[]{:S(2)}) copy-start(bf16[512,1024]{1,0:T(8,128)(2,1)} %down_any.1) | copy-start | bytes 3145732
  5.5 1.0 copy-start.4
  6.6 55.0 %copy-start.1 = (bf16[3,1024,256]{2,1,0:T(8,128)(2,1)S(1)}, bf16[3,1024,256]{2,1,0:T(8,128)(2,1)}, u32[]{:S(2)}) copy-start(bf16[3,1024,256]{2,1,0:T(8,128)(2,1)} %wq_any.1) | copy-start | bytes 4718596
  6.6 55.0 %copy-start.2 = (bf16[1024,512]{1,0:T(8,128)(2,1)S(1)}, bf16[1024,512]{1,0:T(8,128)(2,1)}, u32[]{:S(2)}) copy-start(bf16[1024,512]{1,0:T(8,128)(2,1)} %up_any.1) | copy-start | bytes 3145732
  6.6 55.0 %copy-start.10 = (f32[4]{0:T(128)S(1)}, f32[4]{0:T(128)}, u32[]{:S(2)}) copy-start(f32[4]{0:T(128)} %slope_ref.1) | copy-start | bytes 52
  40.0 1.3 %copy-start = (bf16[4,256,1024]{2,1,0:T(8,128)(2,1)}, bf16[4,256,1024]{2,1,0:T(8,128)(2,1)S(1)}, u32[]{:S(2)}) copy-start(bf16[4,256,1024]{2,1,0:T(8,128)(2,1)S(1)} %get-tuple-element.15.wo_any) | copy-start | bytes 6291460
  41.3 0.7 copy-start.11
  42.0 0.7 copy-start.12

commit v3 on v2

v3 whole, which is shorter than its diff:
```python
import functools

import jax
import jax.numpy as jnp
from jax import lax
from jax.experimental import pallas as pl
from jax.experimental.pallas import tpu as pltpu
from jax.sharding import PartitionSpec as P

MESH = pl.DeviceIdType.MESH
F32, BF16 = jnp.float32, jnp.bfloat16
D = 1024
BLOCK = 128
KEEP = 5
HEAD_ROWS = 16
HEAD_DIM = 64
EPS = 1e-05
DIGIT = 128
LOG2E = 1.4426950408889634
FAR = 1e30
TALL = 160
VMEM_LIMIT = 56 * 1024 * 1024
VMEM = pl.BlockSpec(memory_space=pltpu.VMEM)
SMEM = pl.BlockSpec(memory_space=pltpu.SMEM)
HBM = pl.BlockSpec(memory_space=pltpu.HBM)


def iota(shape, dim):
    return lax.broadcasted_iota(jnp.int32, shape, dim)


def to_row(column):
    n = column.shape[0]
    eye = iota((n, n), 0) == iota((n, n), 1)
    return jnp.sum(jnp.where(eye, column, 0.0), axis=0, keepdims=True)


def to_column(row):
    n = row.shape[1]
    eye = iota((n, n), 0) == iota((n, n), 1)
    return jnp.sum(jnp.where(eye, row, 0.0), axis=1, keepdims=True)


def onehot(mask):
    return jnp.where(mask, 1.0, 0.0).astype(BF16)


def to_blocks(left, right):
    n = left.shape[0] // 8
    return jnp.concatenate([left.reshape(n, 8, 128), right.reshape(n, 8, 128)], axis=1).astype(BF16)


def from_blocks(blocks):
    n = blocks.shape[0]
    wide = blocks.astype(F32)
    return wide[:, :8].reshape(n * 8, 128).astype(BF16), wide[:, 8:].reshape(n * 8, 128).astype(BF16)


def norm_parts(parts, gains):
    total = sum(jnp.sum(p, axis=1, keepdims=True) for p in parts)
    square = sum(jnp.sum(p * p, axis=1, keepdims=True) for p in parts)
    mean = total / D
    scale = lax.rsqrt(square / D - mean * mean + EPS)
    return [((p - mean) * scale * g).astype(BF16) for p, g in zip(parts, gains)]


def final_kernel(in_ref, rows_ref, enc_ref, ctx_ref):
    left, right = from_blocks(in_ref[...])
    here, rows = rows_ref.shape[0], left.shape[0]
    at = iota((here, rows), 1).astype(F32)
    for column, out in ((0, enc_ref), (1, ctx_ref)):
        pick = onehot(at == rows_ref[:, column : column + 1])
        out[:, :128] = jnp.dot(pick, left, preferred_element_type=F32).astype(BF16)
        out[:, 128:] = jnp.dot(pick, right, preferred_element_type=F32).astype(BF16)


class Spot:
    def __init__(self, side):
        self.side = side
        flow = lax.axis_index("flow")
        self.tp = lax.axis_index("tp")
        self.core = lax.rem(flow, 2)
        chip = lax.div(flow, 2)
        self.y = lax.div(chip, side)
        self.z = lax.rem(chip, side)

    def seen(self, core):
        first = core == 0
        return jnp.where(first, self.y, self.z), jnp.where(first, self.z, self.y)

    def device(self, core, a, b, target_core):
        first = core == 0
        a, b = lax.rem(a + self.side, self.side), lax.rem(b + self.side, self.side)
        y, z = jnp.where(first, a, b), jnp.where(first, b, a)
        return ((y * self.side + z) * 2 + target_core, self.tp)

    def beside(self, step):
        parts = lax.axis_size("tp")
        return (lax.axis_index("flow"), lax.rem(self.tp + step + parts, parts))


def remote(src, dst, send, recv, device):
    return pltpu.make_async_remote_copy(
        src_ref=src, dst_ref=dst, send_sem=send, recv_sem=recv, device_id=device, device_id_type=MESH
    )


def started(copy):
    copy.start()
    return copy


class Ring:
    def __init__(self, spot, src, out, send, recv, cut, start=0, rows=None):
        self.me = spot.tp
        self.right, self.left = spot.beside(1), spot.beside(-1)
        self.src, self.out, self.send, self.recv = src, out, send, recv
        rows = src.shape[0] if rows is None else rows
        self.upper, self.lower = pl.ds(start, cut), pl.ds(start + cut, rows - cut)
        parts = lax.axis_size("tp")
        self.before = lax.rem(self.me + parts - 1, parts)
        self.after = lax.rem(self.me + 1, parts)
        self.far = lax.rem(self.me + 2, parts)

    def copy(self, i, block, part, device, own=False):
        src = self.src.at[part] if own and self.src is not None else self.out.at[block, part]
        return remote(src, self.out.at[block, part], self.send.at[i], self.recv.at[i], device)

    def start(self):
        self.first = [
            self.copy(0, self.me, self.upper, self.right, True),
            self.copy(1, self.me, self.lower, self.left, True),
            self.copy(2, self.me, self.lower, self.right, True),
            self.copy(3, self.me, self.upper, self.left, True),
        ]
        for copy in self.first:
            copy.start()

    def forward(self):
        self.copy(0, self.before, self.upper, self.right).wait_recv()
        self.up = self.copy(4, self.before, self.upper, self.right)
        self.up.start()
        self.copy(1, self.after, self.lower, self.left).wait_recv()
        self.down = self.copy(5, self.after, self.lower, self.left)
        self.down.start()

    def finish(self):
        self.copy(2, self.before, self.lower, self.right).wait_recv()
        self.copy(3, self.after, self.upper, self.left).wait_recv()
        self.copy(4, self.far, self.upper, self.right).wait_recv()
        self.copy(5, self.far, self.lower, self.left).wait_recv()
        for copy in (*self.first, self.up, self.down):
            copy.wait_send()


class Sum:
    def __init__(self, spot, terms, relay, pair, one, send, recv, start, rows):
        parts = lax.axis_size("tp")
        self.me = spot.tp
        self.right, self.left = spot.beside(1), spot.beside(-1)
        self.after, self.before, self.far = (lax.rem(self.me + i, parts) for i in (1, parts - 1, 2))
        self.terms, self.relay, self.pair, self.one = terms, relay, pair, one
        self.send, self.recv = send, recv
        self.upper, self.lower = pl.ds(start, rows // 2), pl.ds(start + rows // 2, rows // 2)

    def copy(self, i, src, dst, device):
        copy = remote(src, dst, self.send.at[i], self.recv.at[i], device)
        copy.start()
        return copy

    def start(self):
        terms = self.terms
        self.copies = [
            self.copy(0, terms.at[self.far, self.upper], self.relay.at[0], self.right),
            self.copy(1, terms.at[self.far, self.lower], self.relay.at[1], self.left),
            self.copy(2, terms.at[self.after, self.lower], self.one.at[1], self.right),
            self.copy(3, terms.at[self.before, self.upper], self.one.at[0], self.left),
        ]

    def forward(self):
        for i, (to, rows, device) in enumerate(
            ((self.after, self.upper, self.right), (self.before, self.lower, self.left))
        ):
            self.copies[i].wait_recv()
            self.relay[i] = (self.relay[i].astype(F32) + self.terms[to, rows, :].astype(F32)).astype(BF16)
            self.copies.append(self.copy(4 + i, self.relay.at[i], self.pair.at[i], device))

    def finish(self, keep, out):
        for i in range(2, 6):
            self.copies[i].wait_recv()
        for i, rows in ((0, self.upper), (1, self.lower)):
            terms = self.terms[self.me, rows, :].astype(F32) + self.pair[i].astype(F32) + self.one[i].astype(F32)
            out[rows, :] = (keep[self.me, rows, :].astype(F32) + terms).astype(BF16)
        for copy in self.copies:
            copy.wait_send()


def pack(spot, packets, flow_row, pos_row, holder, first_block):
    side = spot.side
    a, b = spot.seen(spot.core)
    here, flows = packets.shape[0], holder.shape[1]
    rows = 2 * side * side * 8
    flow = to_column(flow_row)
    pos = to_column(pos_row)
    pick = flow == iota((here, flows), 1).astype(F32)
    dest = jnp.sum(jnp.where(pick, holder, 0.0), axis=1, keepdims=True)
    first = jnp.sum(jnp.where(pick, first_block, 0.0), axis=1, keepdims=True)
    code = first * BLOCK + pos + 1.0
    high = jnp.floor(code * (1.0 / DIGIT))
    low = code - high * DIGIT
    before = (dest == to_row(dest)) & (iota((here, here), 0) > iota((here, here), 1))
    rank = jnp.sum(jnp.where(before, 1.0, 0.0), axis=1, keepdims=True)
    chip = jnp.floor(dest * 0.5)
    half = dest - 2.0 * chip
    major = jnp.floor((chip + 0.5) * (1.0 / side))
    minor = chip - major * side
    swap = spot.core == 1

    def ahead(value, mine):
        value = value - mine.astype(F32)
        return jnp.where(value < 0.0, value + side, value)

    a_off = ahead(jnp.where(swap, minor, major), a)
    b_off = ahead(jnp.where(swap, major, minor), b)
    c_off = jnp.abs(half - spot.core.astype(F32))
    base = ((a_off * side + b_off) * 2.0 + c_off) * 8.0
    odd = b_off - 2.0 * jnp.floor(b_off * 0.5)
    spread = (odd * side + a_off) * 8.0 + rank
    base_row, rank_row = to_row(base), to_row(rank)
    sub = iota((rows, here), 0).astype(F32)
    take = onehot(sub == base_row + rank_row)
    take_high = onehot(sub == base_row + 5.0)
    take_low = onehot(sub == base_row + 6.0)
    mine = iota((here, 128), 1).astype(F32) == spread
    left = (
        jnp.dot(take, packets[:, :128], preferred_element_type=F32)
        + jnp.dot(take_high, jnp.where(mine, high, 0.0).astype(BF16), preferred_element_type=F32)
        + jnp.dot(take_low, jnp.where(mine, low, 0.0).astype(BF16), preferred_element_type=F32)
    )
    right = jnp.dot(take, packets[:, 128:], preferred_element_type=F32)
    at = iota((here, 128), 1)
    pool = base + 5.0 + jnp.where(first > 0.0, 1.0, 0.0)
    return to_blocks(left, right), jnp.where(at == 0, base + rank, pool)


def squeeze(rows, padded, turned=False):
    dims = (padded, rows) if turned else (rows, padded)
    row = iota(dims, 1 if turned else 0).astype(F32)
    place = row + (8 - KEEP) * jnp.floor((row + 0.5) * (1.0 / KEEP))
    return onehot(iota(dims, 0 if turned else 1).astype(F32) == place)


def digits(left):
    rows = left.shape[0]
    groups = rows // 128
    r, g = iota((8, rows), 1), iota((8, rows), 0)
    out = []
    for row in (5, 6):
        pick = onehot((r >= g * 128) & (r < g * 128 + 128) & ((r & 7) == row))
        found = jnp.dot(pick, left, preferred_element_type=F32)
        out.append(jnp.concatenate([found[i : i + 1] for i in range(groups)], axis=1))
    return out


def layer_kernel(
    side, slope_ref, pk_any, flow_any, pos_any, holder_any, first_any, gain1_any, gain2_any,
    wq_any, wo_any, up_any, down_any, back_ref, rows_ref,
    pk_ref, flow_ref, pos_ref, holder_ref, first_ref, gain1_ref, gain2_ref, wq_ref, up_ref, down_ref, wo_ref,
    out_box, mid_ref, in_box, rep_ref, mid2_ref,
    all_ref, qkv_ref, far_ref, att_ref, keep_ref, terms_ref, enc_ref, relay, pair, one,
    lsem, s1, r1, s2, r2, s3, r3, s4, r4, wsend, wrecv, asend, arecv, gsend, grecv, ssend, srecv,
):
    spot = Spot(side)
    core, me = spot.core, spot.tp
    other = 1 - core
    a, b = spot.seen(core)
    oa, ob = spot.seen(other)
    rounds, few = 2, side // 2

    barrier = pltpu.get_barrier_semaphore()
    friends = [spot.beside(1), spot.beside(-1), spot.device(core, a, b, other)]
    for i in range(1, side):
        friends += [
            spot.device(core, a + i, b, core), spot.device(core, a, b + i, core),
            spot.device(core, a, b + i, other), spot.device(other, oa, ob + i, other),
        ]
    for device in friends:
        pl.semaphore_signal(barrier, inc=1, device_id=device, device_id_type=MESH)

    sources = (pk_any, flow_any, pos_any, holder_any, first_any, gain1_any, gain2_any, wq_any, up_any, down_any)
    holds = (pk_ref, flow_ref, pos_ref, holder_ref, first_ref, gain1_ref, gain2_ref, wq_ref, up_ref, down_ref)
    loads = [pltpu.make_async_copy(x, h, lsem.at[i]) for i, (x, h) in enumerate(zip(sources, holds))]
    loads.append(pltpu.make_async_copy(wo_any, wo_ref.at[me], lsem.at[len(loads)]))
    for load in loads:
        load.start()
    for load in loads[:7]:
        load.wait()
    flow_row, pos_row, holder, first_block = (
        ref[...].astype(F32)[None] for ref in (flow_ref, pos_ref, holder_ref, first_ref)
    )
    mine = holder == lax.axis_index("flow").astype(F32)
    edge = jnp.max(jnp.where(mine, first_block, 0.0), axis=1, keepdims=True) * BLOCK
    blocks, found = pack(spot, pk_ref[...], flow_row, pos_row, holder, first_block)
    out_box[...] = blocks.reshape(out_box.shape)
    rows_ref[...] = found
    parts, width = all_ref.shape[0], all_ref.shape[2]
    gain_rows = jnp.where(
        iota((HEAD_ROWS, width), 0) == 0, gain1_ref[...].astype(F32)[None], gain2_ref[...].astype(F32)[None]
    ).astype(BF16)
    all_ref[me, :HEAD_ROWS, :] = gain_rows
    pl.semaphore_wait(barrier, len(friends))

    def hop1(h):
        some = pl.ds(h * few, few)
        return [
            started(
                remote(out_box.at[i, some], mid_ref.at[i, some], s1.at[h, i], r1.at[h, i],
                       spot.device(core, a + i, b, core))
            )
            for i in range(1, side)
        ]

    def hop2(h):
        return [
            started(
                remote(mid_ref.at[:, h * few + i, t], in_box.at[h, t, i], s2.at[h, i, t], r2.at[h, i, t],
                       spot.device(core, a, b + h * few + i, core if t == 0 else other))
            )
            for i in range(few) for t in range(2) if h or i or t
        ]

    first = [hop1(0)]
    weights = Ring(spot, wo_any, wo_ref, wsend, wrecv, wo_any.shape[0] // 2)
    weights.start()
    mid_ref[0] = out_box[0]
    for copy in first[0]:
        copy.wait_recv()
    second = [hop2(0)]
    first.append(hop1(1))
    in_box[0, 0, 0] = mid_ref[:, 0, 0]
    for copy in first[1]:
        copy.wait_recv()
    second.append(hop2(1))
    weights.forward()

    sources_here = side * side
    rows = sources_here * KEEP
    total = rounds * rows
    rings, high, low = [], [], []
    for h in range(rounds):
        for copy in second[h]:
            copy.wait_recv()
        left, right = from_blocks(in_box[h].reshape(sources_here, 16, 128))
        keep = squeeze(rows, sources_here * 8)
        here = pl.ds(HEAD_ROWS + h * rows, rows)
        all_ref[me, here, :128] = jnp.dot(keep, left, preferred_element_type=F32).astype(BF16)
        all_ref[me, here, 128:] = jnp.dot(keep, right, preferred_element_type=F32).astype(BF16)
        begin = HEAD_ROWS * (h > 0) + h * rows
        rings.append(
            Ring(spot, None, all_ref, asend.at[h], arecv.at[h], rows // 2, begin, rows + HEAD_ROWS * (h == 0))
        )
        rings[h].start()
        found = digits(left)
        high.append(found[0])
        low.append(found[1])
    both = jnp.where(
        iota((8, total // KEEP * 8), 0) == 0, jnp.concatenate(high, axis=1), jnp.concatenate(low, axis=1)
    ).astype(BF16)
    keep = squeeze(total, total // KEEP * 8)
    across = (((1,), (1,)), ((), ()))
    by_row = lax.dot_general(both, keep, across, preferred_element_type=F32)
    by_column = lax.dot_general(keep, both, across, preferred_element_type=F32)
    slot_row = by_row[0:1] * DIGIT + by_row[1:2] - 1.0
    slot_column = by_column[:, 0:1] * DIGIT + by_column[:, 1:2] - 1.0
    tag_row = jnp.where(slot_row >= edge, 1.0, 0.0)
    tag_column = jnp.where(slot_column >= edge, 1.0, 0.0)

    rings[0].forward()
    loads[7].wait()
    gains = None
    for h in range(rounds):
        if h + 1 < rounds:
            rings[h + 1].forward()
        rings[h].finish()
        if gains is None:
            gains = [all_ref[p, :HEAD_ROWS, :].astype(F32) for p in range(parts)]
        here = pl.ds(HEAD_ROWS + h * rows, rows)
        normed = jnp.concatenate(
            norm_parts([all_ref[p, here, :].astype(F32) for p in range(parts)], [g[0:1] for g in gains]), axis=1
        )
        for k in range(3):
            qkv_ref[k, pl.ds(h * rows, rows), :] = jnp.dot(normed, wq_ref[k], preferred_element_type=F32).astype(BF16)

    def attend(chunk):
        rows = pl.ds(chunk * TALL, TALL)
        part = slice(chunk * TALL, (chunk + 1) * TALL)
        itself = iota((TALL, total), 0) + chunk * TALL == iota((TALL, total), 1)
        allowed = ((tag_column[part] == tag_row) & (slot_row >= 0.0)) | itself
        far_ref[...] = jnp.where(allowed, jnp.abs(slot_column[part] - slot_row) * LOG2E, FAR)
        first = iota((TALL, 128), 1) < HEAD_DIM
        for two in range(width // 128):
            cols = slice(two * 128, (two + 1) * 128)
            query = qkv_ref[0, rows, cols]
            keys, values = qkv_ref[1, :, cols], qkv_ref[2, :, cols]
            halves = []
            for half in range(2):
                mine = jnp.where(first == (half == 0), query, jnp.zeros_like(query))
                scores = lax.dot_general(mine, keys, across, preferred_element_type=F32)
                weights = jnp.exp2(
                    scores * (HEAD_DIM**-0.5 * LOG2E) - slope_ref[2 * two + half] * far_ref[...]
                )
                probs = weights * (1.0 / jnp.sum(weights, axis=1, keepdims=True))
                halves.append(jnp.dot(probs.astype(BF16), values, preferred_element_type=F32))
            att_ref[me, rows, cols] = jnp.where(first, halves[0], halves[1]).astype(BF16)

    def forward_layer(chunk):
        rows = pl.ds(chunk * TALL, TALL)
        there = pl.ds(HEAD_ROWS + chunk * TALL, TALL)
        attn = sum(
            jnp.dot(att_ref[p, rows, :], wo_ref[p], preferred_element_type=F32).astype(BF16).astype(F32)
            for p in range(parts)
        )
        middle = [
            (all_ref[p, there, :].astype(F32) + attn[:, p * width : (p + 1) * width]).astype(BF16)
            for p in range(parts)
        ]
        for p in range(parts):
            keep_ref[p, rows, :] = middle[p]
        normed = jnp.concatenate(norm_parts([m.astype(F32) for m in middle], [g[1:2] for g in gains]), axis=1)
        upward = jnp.dot(normed, up_ref[...], preferred_element_type=F32)
        active = (0.5 * upward * (1.0 + lax.erf(upward * (0.5**0.5)))).astype(BF16)
        for p in range(parts):
            terms_ref[p, rows, :] = jnp.dot(
                active, down_ref[:, p * width : (p + 1) * width], preferred_element_type=F32
            ).astype(BF16)

    chunks = total // TALL
    rings = [Ring(spot, None, att_ref, gsend.at[c], grecv.at[c], TALL // 2, c * TALL, TALL) for c in range(chunks)]
    sums = [
        Sum(spot, terms_ref, relay.at[c], pair.at[c], one.at[c], ssend.at[c], srecv.at[c], c * TALL, TALL)
        for c in range(chunks)
    ]
    for c in range(chunks):
        attend(c)
        rings[c].start()
        if c:
            rings[c - 1].forward()
    weights.finish()
    for load in loads[8:]:
        load.wait()
    for c in range(chunks):
        if c == 1:
            rings[chunks - 1].forward()
        rings[c].finish()
        forward_layer(c)
        sums[c].start()
        if c:
            sums[c - 1].forward()
    sums[chunks - 1].forward()
    for c in range(chunks):
        sums[c].finish(keep_ref, enc_ref)

    encoded = enc_ref[...]
    number = iota((8, total), 0).astype(F32)
    members = jnp.where((slot_row >= 0.0) & (tag_row == number), 1.0, 0.0)
    counts = jnp.sum(members, axis=1, keepdims=True)
    pooled = jnp.dot(members.astype(BF16), encoded, preferred_element_type=F32) / counts
    wide = jnp.dot(squeeze(total, total // KEEP * 8, True), encoded, preferred_element_type=F32)
    sub = iota(wide.shape, 0) & 7
    wide = jnp.where(sub == 5, pooled[0:1], jnp.where(sub == 6, pooled[1:2], wide))
    rep_ref[...] = to_blocks(wide[:, :128], wide[:, 128:]).reshape(rep_ref.shape)

    third = []
    for h in range(rounds):
        for i in range(few):
            for t in range(2):
                if h or i or t:
                    frame, fa, fb = (core, a, b) if t == 0 else (other, oa, ob)
                    far = h * few + i
                    third.append(
                        started(
                            remote(rep_ref.at[h, t, i], mid2_ref.at[:, far, t], s3.at[far, t], r3.at[far, t],
                                   spot.device(frame, fa, fb - far, frame))
                        )
                    )
    mid2_ref[:, 0, 0] = rep_ref[0, 0, 0]
    for copy in third:
        copy.wait_recv()
    fourth = [
        started(remote(mid2_ref.at[i], back_ref.at[i], s4.at[i], r4.at[i], spot.device(core, a - i, b, core)))
        for i in range(1, side)
    ]
    back_ref[0] = mid2_ref[0]
    for copy in fourth:
        copy.wait_recv()
    for copy in (*first[0], *first[1], *second[0], *second[1], *third, *fourth):
        copy.wait_send()


def shape(*dims, dtype=BF16):
    return jax.ShapeDtypeStruct(dims, dtype)


def local(kernel, outs, specs, scratch=()):
    return pl.pallas_call(
        kernel,
        out_shape=outs,
        in_specs=specs,
        out_specs=jax.tree.map(lambda _: VMEM, outs),
        scratch_shapes=list(scratch),
        compiler_params=pltpu.CompilerParams(vmem_limit_bytes=VMEM_LIMIT),
    )


def linked(kernel, outs, inputs, scratch, number):
    return pl.pallas_call(
        kernel,
        out_shape=outs,
        in_specs=[VMEM] * inputs if isinstance(inputs, int) else inputs,
        out_specs=jax.tree.map(lambda _: VMEM, outs),
        scratch_shapes=scratch,
        compiler_params=pltpu.CompilerParams(
            vmem_limit_bytes=VMEM_LIMIT, collective_id=number, has_side_effects=True
        ),
    )


def dma(*dims):
    return pltpu.SemaphoreType.DMA(dims)


def on_device(
    packets, packet_flow, packet_pos, flow_holder_rank, flow_first_block,
    w_qkv, w_out, w_up, w_down, gain_first, gain_second, head_slopes,
):
    owners, parts = lax.axis_size("flow"), lax.axis_size("tp")
    side = int(round((owners // 2) ** 0.5))
    here, width = packets.shape
    total = owners * KEEP
    chunks = total // TALL
    given = (packets, packet_flow, packet_pos, flow_holder_rank, flow_first_block, gain_first, gain_second)
    box, turned = (side, side, 2, 16, 128), (2, 2, side // 2, side, 16, 128)

    def hold(*dims):
        return pltpu.VMEM(dims, BF16)

    some = hold(chunks, 2, TALL // 2, width)
    full = hold(parts, total, width)
    back, rows = linked(
        functools.partial(layer_kernel, side),
        (shape(*box), shape(here, 128, dtype=F32)),
        [SMEM] + [HBM] * 11,
        [
            *(pltpu.VMEM(v.shape, v.dtype) for v in (*given, w_qkv, w_up, w_down)), hold(parts, *w_out.shape),
            hold(*box), hold(*box), hold(*turned), hold(*turned), hold(*box),
            hold(parts, HEAD_ROWS + total, width), hold(3, total, width), pltpu.VMEM((TALL, total), F32),
            full, full, full, hold(total, width), some, some, some,
            dma(11), dma(2, side), dma(2, side), dma(2, side // 2, 2), dma(2, side // 2, 2),
            dma(side, 2), dma(side, 2), dma(side), dma(side), dma(6), dma(6), dma(2, 6), dma(2, 6),
            dma(chunks, 6), dma(chunks, 6), dma(chunks, 6), dma(chunks, 6),
        ],
        1,
    )(head_slopes, *given, w_qkv, w_out, w_up, w_down)

    return local(final_kernel, (shape(here, width), shape(here, width)), [VMEM] * 2)(
        back.reshape(owners, 16, 128), rows
    )


def solution(mesh):
    return jax.shard_map(
        on_device,
        mesh=mesh,
        in_specs=(
            P("flow", "tp"),
            P("flow"),
            P("flow"),
            P(),
            P(),
            P(None, None, "tp"),
            P("tp", None),
            P(None, "tp"),
            P("tp", None),
            P("tp"),
            P("tp"),
            P("tp"),
        ),
        out_specs=(P("flow", "tp"), P("flow", "tp")),
        check_vma=False,
    )
```

time: 124 us -> 100 us (0.81)
  Pallas kernels: 116 us -> 99 us
  local copies, waits for them, and re-layouts: 7.3 us -> 0 us
    pallas_call x7 -> x1, Pallas kernels: 114 us -> 96.5 us  [on_device(): linked(functools.partial(layer_kernel, side), (shape(*box), shape(here, 1...]
    unnamed x26 -> x0, local copies, waits for them, and re-layouts: 7.3 us -> none
where the time goes in v3:
time: 100 us; the launch traced here: 99.6 us
  Pallas kernels  99 us (99%)
    pallas_call x1, Pallas kernels, on_device(): linked(functools.partial(layer_kernel, side), (shape(*box), shape(here, 1...  96.5 us
    pallas_call x1, Pallas kernels, on_device(): local(final_kernel, (shape(here, width), shape(here, width)), [VMEM] * 2)  2.5 us

profile of v3, /device:TPU:1, one launch (start us, length us, event | category | flops | bytes accessed | tf_op | source)
XLA Modules:
  0.0 99.6 jit_solution(6130675680847269100)
XLA Ops:
  0.6 96.5 %shard_map.131 = (bf16[8,8,2,16,128]{4,3,2,1,0:T(8,128)(2,1)}, f32[256,128]{1,0:T(8,128)}) custom-call(f32[4]{0:T(128)} %slope_ref.1, bf16[256,256]{1,0:T(8,128)(2,1)} %pk_any.1, s32[256]{0:T(256)} %flow_any.1, s32[256]{0:T(256)} %pos_any.1, s32[256]{0:T(256)} %holder_any.1, s32[256]{0:T(256)} %first_any.1, bf16[256]{0:T(256)(128)(2,1)} %gain1_any.1, ...), custom_call_target="tpu_custom_call" | custom-call | tf_op jit(solution)/shard_map/pallas_call | solution.py:549
  97.2 2.5 %shard_map.132 = (bf16[256,256]{1,0:T(8,128)(2,1)}, bf16[256,256]{1,0:T(8,128)(2,1)}) custom-call(bf16[128,16,128]{2,1,0:T(8,128)(2,1)} %bitcast.1, f32[256,128]{1,0:T(8,128)} %get-tuple-element.5.rows_ref), custom_call_target="tpu_custom_call" | custom-call | tf_op jit(solution)/shard_map/pallas_call | solution.py:565

commit v4 on v3

--- a/solution.py
+++ b/solution.py
@@ -64,14 +64,18 @@
     return [((p - mean) * scale * g).astype(BF16) for p, g in zip(parts, gains)]
 
 
-def final_kernel(in_ref, rows_ref, enc_ref, ctx_ref):
+def final_kernel(in_ref, pool_ref, rows_ref, enc_ref, ctx_ref):
     left, right = from_blocks(in_ref[...])
     here, rows = rows_ref.shape[0], left.shape[0]
-    at = iota((here, rows), 1).astype(F32)
-    for column, out in ((0, enc_ref), (1, ctx_ref)):
-        pick = onehot(at == rows_ref[:, column : column + 1])
-        out[:, :128] = jnp.dot(pick, left, preferred_element_type=F32).astype(BF16)
-        out[:, 128:] = jnp.dot(pick, right, preferred_element_type=F32).astype(BF16)
+    pick = onehot(iota((here, rows), 1).astype(F32) == rows_ref[:, 0:1])
+    enc_ref[:, :128] = jnp.dot(pick, left, preferred_element_type=F32).astype(BF16)
+    enc_ref[:, 128:] = jnp.dot(pick, right, preferred_element_type=F32).astype(BF16)
+    pool = pool_ref[...]
+    at = iota((here, pool.shape[0]), 1).astype(F32)
+    for half in range(2):
+        pick = onehot(at == rows_ref[:, 1:2] + float(half))
+        cols = slice(half * 128, (half + 1) * 128)
+        ctx_ref[:, cols] = jnp.dot(pick, pool, preferred_element_type=F32).astype(BF16)
 
 
 class Spot:
@@ -239,7 +243,7 @@
     )
     right = jnp.dot(take, packets[:, 128:], preferred_element_type=F32)
     at = iota((here, 128), 1)
-    pool = base + 5.0 + jnp.where(first > 0.0, 1.0, 0.0)
+    pool = base * 0.5 + jnp.where(first > 0.0, 2.0, 0.0)
     return to_blocks(left, right), jnp.where(at == 0, base + rank, pool)
 
 
@@ -264,11 +268,11 @@
 
 def layer_kernel(
     side, slope_ref, pk_any, flow_any, pos_any, holder_any, first_any, gain1_any, gain2_any,
-    wq_any, wo_any, up_any, down_any, back_ref, rows_ref,
+    wq_any, wo_any, up_any, down_any, back_ref, pool_ref, rows_ref,
     pk_ref, flow_ref, pos_ref, holder_ref, first_ref, gain1_ref, gain2_ref, wq_ref, up_ref, down_ref, wo_ref,
-    out_box, mid_ref, in_box, rep_ref, mid2_ref,
+    out_box, mid_ref, in_box, rep_ref, mid2_ref, pool_out, pool_mid, pool_pack,
     all_ref, qkv_ref, far_ref, att_ref, keep_ref, terms_ref, enc_ref, relay, pair, one,
-    lsem, s1, r1, s2, r2, s3, r3, s4, r4, wsend, wrecv, asend, arecv, gsend, grecv, ssend, srecv,
+    lsem, s1, r1, s2, r2, s3, r3, s4, r4, s5, r5, s6, r6, wsend, wrecv, asend, arecv, gsend, grecv, ssend, srecv,
 ):
     spot = Spot(side)
     core, me = spot.core, spot.tp
@@ -445,6 +449,43 @@
         rings[c].start()
         if c:
             rings[c - 1].forward()
+    third, fourth, moved = [[] for _ in range(rounds)], [], []
+
+    def toward(far, t):
+        frame, fa, fb = (core, a, b) if t == 0 else (other, oa, ob)
+        return spot.device(frame, fa, fb - far, frame)
+
+    def reply(c):
+        sums[c].finish(keep_ref, enc_ref)
+        h, t = c // 2, c % 2
+        spread = squeeze(TALL, TALL // KEEP * 8, True)
+        wide = jnp.dot(spread, enc_ref[pl.ds(c * TALL, TALL), :], preferred_element_type=F32)
+        rep_ref[h, t] = to_blocks(wide[:, :128], wide[:, 128:]).reshape(few, side, 16, 128)
+        for i in range(few):
+            far = h * few + i
+            if far or t:
+                third[h].append(
+                    started(
+                        remote(rep_ref.at[h, t, i], mid2_ref.at[:, far, t], s3.at[far, t], r3.at[far, t],
+                               toward(far, t))
+                    )
+                )
+            else:
+                mid2_ref[:, 0, 0] = rep_ref[0, 0, 0]
+
+    def relay_back(h):
+        for copy in third[h]:
+            copy.wait_recv()
+        some = pl.ds(h * few, few)
+        for i in range(1, side):
+            fourth.append(
+                started(
+                    remote(mid2_ref.at[i, some], back_ref.at[i, some], s4.at[h, i], r4.at[h, i],
+                           spot.device(core, a - i, b, core))
+                )
+            )
+        back_ref[0, some] = mid2_ref[0, some]
+
     weights.finish()
     for load in loads[8:]:
         load.wait()
@@ -456,44 +497,47 @@
         sums[c].start()
         if c:
             sums[c - 1].forward()
-    sums[chunks - 1].forward()
-    for c in range(chunks):
-        sums[c].finish(keep_ref, enc_ref)
+    reply(0)
+    reply(1)
+    sums[3].forward()
+    reply(2)
+    relay_back(0)
+    reply(3)
 
     encoded = enc_ref[...]
     number = iota((8, total), 0).astype(F32)
     members = jnp.where((slot_row >= 0.0) & (tag_row == number), 1.0, 0.0)
     counts = jnp.sum(members, axis=1, keepdims=True)
     pooled = jnp.dot(members.astype(BF16), encoded, preferred_element_type=F32) / counts
-    wide = jnp.dot(squeeze(total, total // KEEP * 8, True), encoded, preferred_element_type=F32)
-    sub = iota(wide.shape, 0) & 7
-    wide = jnp.where(sub == 5, pooled[0:1], jnp.where(sub == 6, pooled[1:2], wide))
-    rep_ref[...] = to_blocks(wide[:, :128], wide[:, 128:]).reshape(rep_ref.shape)
-
-    third = []
-    for h in range(rounds):
-        for i in range(few):
-            for t in range(2):
-                if h or i or t:
-                    frame, fa, fb = (core, a, b) if t == 0 else (other, oa, ob)
-                    far = h * few + i
-                    third.append(
-                        started(
-                            remote(rep_ref.at[h, t, i], mid2_ref.at[:, far, t], s3.at[far, t], r3.at[far, t],
-                                   spot.device(frame, fa, fb - far, frame))
-                        )
-                    )
-    mid2_ref[:, 0, 0] = rep_ref[0, 0, 0]
-    for copy in third:
+    lane = iota((16, 128), 0)
+    four = [
+        jnp.where((lane & 2) == 0, pooled[0:1, cols], pooled[1:2, cols]) for cols in (slice(0, 128), slice(128, 256))
+    ]
+    pool_out[...] = jnp.where((lane & 1) == 0, four[0], four[1]).astype(BF16)
+    for far in range(side):
+        for t in range(2):
+            if far or t:
+                moved.append(
+                    started(remote(pool_out, pool_mid.at[far, t], s5.at[far, t], r5.at[far, t], toward(far, t)))
+                )
+    pool_mid[0, 0] = pool_out[...]
+    relay_back(1)
+    for copy in moved:
         copy.wait_recv()
-    fourth = [
-        started(remote(mid2_ref.at[i], back_ref.at[i], s4.at[i], r4.at[i], spot.device(core, a - i, b, core)))
+    quarter = lax.shift_right_logical(iota((side // 2, 16, 128), 1), 2)
+    grouped = pool_mid[...].astype(F32).reshape(side // 2, 4, 16, 128)
+    packed = grouped[:, 0]
+    for i in range(1, 4):
+        packed = jnp.where(quarter == i, grouped[:, i], packed)
+    pool_pack[...] = packed.astype(BF16)
+    last = [
+        started(remote(pool_pack, pool_ref.at[i], s6.at[i], r6.at[i], spot.device(core, a - i, b, core)))
         for i in range(1, side)
     ]
-    back_ref[0] = mid2_ref[0]
-    for copy in fourth:
+    pool_ref[0] = pool_pack[...]
+    for copy in (*fourth, *last):
         copy.wait_recv()
-    for copy in (*first[0], *first[1], *second[0], *second[1], *third, *fourth):
+    for copy in (*first[0], *first[1], *second[0], *second[1], *third[0], *third[1], *fourth, *moved, *last):
         copy.wait_send()
 
 
@@ -546,24 +590,25 @@
 
     some = hold(chunks, 2, TALL // 2, width)
     full = hold(parts, total, width)
-    back, rows = linked(
+    back, pool, rows = linked(
         functools.partial(layer_kernel, side),
-        (shape(*box), shape(here, 128, dtype=F32)),
+        (shape(*box), shape(side, side // 2, 16, 128), shape(here, 128, dtype=F32)),
         [SMEM] + [HBM] * 11,
         [
             *(pltpu.VMEM(v.shape, v.dtype) for v in (*given, w_qkv, w_up, w_down)), hold(parts, *w_out.shape),
             hold(*box), hold(*box), hold(*turned), hold(*turned), hold(*box),
+            hold(16, 128), hold(side, 2, 16, 128), hold(side // 2, 16, 128),
             hold(parts, HEAD_ROWS + total, width), hold(3, total, width), pltpu.VMEM((TALL, total), F32),
             full, full, full, hold(total, width), some, some, some,
             dma(11), dma(2, side), dma(2, side), dma(2, side // 2, 2), dma(2, side // 2, 2),
-            dma(side, 2), dma(side, 2), dma(side), dma(side), dma(6), dma(6), dma(2, 6), dma(2, 6),
+            dma(side, 2), dma(side, 2), dma(2, side), dma(2, side), dma(side, 2), dma(side, 2), dma(side), dma(side), dma(6), dma(6), dma(2, 6), dma(2, 6),
             dma(chunks, 6), dma(chunks, 6), dma(chunks, 6), dma(chunks, 6),
         ],
         1,
     )(head_slopes, *given, w_qkv, w_out, w_up, w_down)
 
-    return local(final_kernel, (shape(here, width), shape(here, width)), [VMEM] * 2)(
-        back.reshape(owners, 16, 128), rows
+    return local(final_kernel, (shape(here, width), shape(here, width)), [VMEM] * 3)(
+        back.reshape(owners, 16, 128), pool.reshape(owners * 4, 128), rows
     )
 
 

time: 100 us -> 103 us (1.030)
  Pallas kernels: 99 us -> 102 us
    pallas_call x2, Pallas kernels: 99 us -> 102 us  [the longest x1 99.2 us: on_device(): linked(functools.partial(layer_kernel, side), (shape(*box), shape(side, s...]
where the time goes in v4:
time: 103 us; the launch traced here: 102 us
  Pallas kernels  102 us (99%)
    pallas_call x1, Pallas kernels, on_device(): linked(functools.partial(layer_kernel, side), (shape(*box), shape(side, s...  99.2 us
    pallas_call x1, Pallas kernels, on_device(): local(final_kernel, (shape(here, width), shape(here, width)), [VMEM] * 3)  2.43 us

profile of v4, /device:TPU:1, one launch (start us, length us, event | category | flops | bytes accessed | tf_op | source)
XLA Modules:
  0.0 102.2 jit_solution(4947063938997446505)
XLA Ops:
  0.6 99.2 %shard_map.131 = (bf16[8,8,2,16,128]{4,3,2,1,0:T(8,128)(2,1)}, bf16[8,4,16,128]{3,2,1,0:T(8,128)(2,1)}, f32[256,128]{1,0:T(8,128)}) custom-call(f32[4]{0:T(128)} %slope_ref.1, bf16[256,256]{1,0:T(8,128)(2,1)} %pk_any.1, s32[256]{0:T(256)} %flow_any.1, s32[256]{0:T(256)} %pos_any.1, s32[256]{0:T(256)} %holder_any.1, s32[256]{0:T(256)} %first_any.1, ...), custom_call_target="tpu_custom_call" | custom-call | tf_op jit(solution)/shard_map/pallas_call | solution.py:593
  99.8 2.4 %shard_map.132 = (bf16[256,256]{1,0:T(8,128)(2,1)}, bf16[256,256]{1,0:T(8,128)(2,1)}) custom-call(bf16[128,16,128]{2,1,0:T(8,128)(2,1)} %bitcast.2, bf16[512,128]{1,0:T(8,128)(2,1)} %bitcast.3, f32[256,128]{1,0:T(8,128)} %get-tuple-element.7.rows_ref), custom_call_target="tpu_custom_call" | custom-call | tf_op jit(solution)/shard_map/pallas_call | solution.py:610

commit v5 on v3

--- a/solution.py
+++ b/solution.py
@@ -65,13 +65,11 @@
 
 
 def final_kernel(in_ref, rows_ref, enc_ref, ctx_ref):
-    left, right = from_blocks(in_ref[...])
-    here, rows = rows_ref.shape[0], left.shape[0]
-    at = iota((here, rows), 1).astype(F32)
+    given = jnp.concatenate(from_blocks(in_ref[...]), axis=1)
+    at = iota((rows_ref.shape[0], given.shape[0]), 1).astype(F32)
     for column, out in ((0, enc_ref), (1, ctx_ref)):
         pick = onehot(at == rows_ref[:, column : column + 1])
-        out[:, :128] = jnp.dot(pick, left, preferred_element_type=F32).astype(BF16)
-        out[:, 128:] = jnp.dot(pick, right, preferred_element_type=F32).astype(BF16)
+        out[...] = jnp.dot(pick, given, preferred_element_type=F32).astype(BF16)
 
 
 class Spot:
@@ -284,14 +282,18 @@
             spot.device(core, a + i, b, core), spot.device(core, a, b + i, core),
             spot.device(core, a, b + i, other), spot.device(other, oa, ob + i, other),
         ]
-    for device in friends:
-        pl.semaphore_signal(barrier, inc=1, device_id=device, device_id_type=MESH)
-
     sources = (pk_any, flow_any, pos_any, holder_any, first_any, gain1_any, gain2_any, wq_any, up_any, down_any)
     holds = (pk_ref, flow_ref, pos_ref, holder_ref, first_ref, gain1_ref, gain2_ref, wq_ref, up_ref, down_ref)
     loads = [pltpu.make_async_copy(x, h, lsem.at[i]) for i, (x, h) in enumerate(zip(sources, holds))]
-    loads.append(pltpu.make_async_copy(wo_any, wo_ref.at[me], lsem.at[len(loads)]))
-    for load in loads:
+    share = wo_any.shape[0] // 2
+    begin = pl.multiple_of(core * share, share)
+    our = pl.ds(begin, share)
+    loads.append(pltpu.make_async_copy(wo_any.at[our], wo_ref.at[me, our], lsem.at[len(loads)]))
+    for load in loads[:7]:
+        load.start()
+    for device in friends:
+        pl.semaphore_signal(barrier, inc=1, device_id=device, device_id_type=MESH)
+    for load in loads[7:]:
         load.start()
     for load in loads[:7]:
         load.wait()
@@ -329,19 +331,23 @@
             for i in range(few) for t in range(2) if h or i or t
         ]
 
-    first = [hop1(0)]
-    weights = Ring(spot, wo_any, wo_ref, wsend, wrecv, wo_any.shape[0] // 2)
+    first = [hop1(0), hop1(1)]
+    weights = Ring(spot, wo_any, wo_ref, wsend, wrecv, share // 2, begin, share)
     weights.start()
     mid_ref[0] = out_box[0]
     for copy in first[0]:
         copy.wait_recv()
     second = [hop2(0)]
-    first.append(hop1(1))
     in_box[0, 0, 0] = mid_ref[:, 0, 0]
+    weights.forward()
     for copy in first[1]:
         copy.wait_recv()
     second.append(hop2(1))
-    weights.forward()
+    weights.finish()
+    loads[10].wait()
+    swap = started(
+        remote(wo_ref.at[:, our], wo_ref.at[:, our], wsend.at[6], wrecv.at[6], spot.device(core, a, b, other))
+    )
 
     sources_here = side * side
     rows = sources_here * KEEP
@@ -391,6 +397,10 @@
         for k in range(3):
             qkv_ref[k, pl.ds(h * rows, rows), :] = jnp.dot(normed, wq_ref[k], preferred_element_type=F32).astype(BF16)
 
+    number = iota((8, total), 0).astype(F32)
+    members = jnp.where((slot_row >= 0.0) & (tag_row == number), 1.0, 0.0)
+    counts = jnp.sum(members, axis=1, keepdims=True)
+
     def attend(chunk):
         rows = pl.ds(chunk * TALL, TALL)
         part = slice(chunk * TALL, (chunk + 1) * TALL)
@@ -445,8 +455,11 @@
         rings[c].start()
         if c:
             rings[c - 1].forward()
-    weights.finish()
-    for load in loads[8:]:
+    theirs = pl.ds(pl.multiple_of(other * share, share), share)
+    remote(
+        wo_ref.at[:, theirs], wo_ref.at[:, theirs], wsend.at[6], wrecv.at[6], spot.device(core, a, b, other)
+    ).wait_recv()
+    for load in loads[8:10]:
         load.wait()
     for c in range(chunks):
         if c == 1:
@@ -456,44 +469,55 @@
         sums[c].start()
         if c:
             sums[c - 1].forward()
+    expand = squeeze(TALL, TALL // KEEP * 8, True)
+
+    def settle(c):
+        sums[c].finish(keep_ref, enc_ref)
+        wide = jnp.dot(expand, enc_ref[pl.ds(c * TALL, TALL), :], preferred_element_type=F32)
+        rep_ref[c // 2, c % 2] = to_blocks(wide[:, :128], wide[:, 128:]).reshape(few, side, 16, 128)
+
+    settle(0)
+    settle(1)
     sums[chunks - 1].forward()
-    for c in range(chunks):
-        sums[c].finish(keep_ref, enc_ref)
-
-    encoded = enc_ref[...]
-    number = iota((8, total), 0).astype(F32)
-    members = jnp.where((slot_row >= 0.0) & (tag_row == number), 1.0, 0.0)
-    counts = jnp.sum(members, axis=1, keepdims=True)
-    pooled = jnp.dot(members.astype(BF16), encoded, preferred_element_type=F32) / counts
-    wide = jnp.dot(squeeze(total, total // KEEP * 8, True), encoded, preferred_element_type=F32)
-    sub = iota(wide.shape, 0) & 7
-    wide = jnp.where(sub == 5, pooled[0:1], jnp.where(sub == 6, pooled[1:2], wide))
-    rep_ref[...] = to_blocks(wide[:, :128], wide[:, 128:]).reshape(rep_ref.shape)
-
-    third = []
+    settle(2)
+    settle(3)
+
+    pooled = jnp.dot(members.astype(BF16), enc_ref[...], preferred_element_type=F32) / counts
+    line = iota((16, 128), 0)
+    near = jnp.where(line < 8, pooled[0:1, :128], pooled[0:1, 128:])
+    next_to = jnp.where(line < 8, pooled[1:2, :128], pooled[1:2, 128:])
+    tile = jnp.where((line & 7) == 5, near, jnp.where((line & 7) == 6, next_to, 0.0)).astype(BF16)
+    rep_ref[...] = rep_ref[...] + tile
+
+    third, fourth = [[] for _ in range(rounds)], []
     for h in range(rounds):
         for i in range(few):
             for t in range(2):
                 if h or i or t:
                     frame, fa, fb = (core, a, b) if t == 0 else (other, oa, ob)
                     far = h * few + i
-                    third.append(
+                    third[h].append(
                         started(
                             remote(rep_ref.at[h, t, i], mid2_ref.at[:, far, t], s3.at[far, t], r3.at[far, t],
                                    spot.device(frame, fa, fb - far, frame))
                         )
                     )
     mid2_ref[:, 0, 0] = rep_ref[0, 0, 0]
-    for copy in third:
-        copy.wait_recv()
-    fourth = [
-        started(remote(mid2_ref.at[i], back_ref.at[i], s4.at[i], r4.at[i], spot.device(core, a - i, b, core)))
-        for i in range(1, side)
-    ]
-    back_ref[0] = mid2_ref[0]
+    for h in range(rounds):
+        for copy in third[h]:
+            copy.wait_recv()
+        some = pl.ds(h * few, few)
+        for i in range(1, side):
+            fourth.append(
+                started(
+                    remote(mid2_ref.at[i, some], back_ref.at[i, some], s4.at[h, i], r4.at[h, i],
+                           spot.device(core, a - i, b, core))
+                )
+            )
+        back_ref[0, some] = mid2_ref[0, some]
     for copy in fourth:
         copy.wait_recv()
-    for copy in (*first[0], *first[1], *second[0], *second[1], *third, *fourth):
+    for copy in (*first[0], *first[1], *second[0], *second[1], *third[0], *third[1], *fourth, swap):
         copy.wait_send()
 
 
@@ -556,7 +580,7 @@
             hold(parts, HEAD_ROWS + total, width), hold(3, total, width), pltpu.VMEM((TALL, total), F32),
             full, full, full, hold(total, width), some, some, some,
             dma(11), dma(2, side), dma(2, side), dma(2, side // 2, 2), dma(2, side // 2, 2),
-            dma(side, 2), dma(side, 2), dma(side), dma(side), dma(6), dma(6), dma(2, 6), dma(2, 6),
+            dma(side, 2), dma(side, 2), dma(2, side), dma(2, side), dma(7), dma(7), dma(2, 6), dma(2, 6),
             dma(chunks, 6), dma(chunks, 6), dma(chunks, 6), dma(chunks, 6),
         ],
         1,

time: 100 us -> 93.1 us (0.931)
  Pallas kernels: 99 us -> 91.7 us
    pallas_call x1, Pallas kernels: 96.5 us -> 89.4 us  [on_device(): linked(functools.partial(layer_kernel, side), (shape(*box), shape(here, 1...]
where the time goes in v5:
time: 93.1 us; the launch traced here: 92.3 us
  Pallas kernels  91.7 us (98%)
    pallas_call x1, Pallas kernels, on_device(): linked(functools.partial(layer_kernel, side), (shape(*box), shape(here, 1...  89.4 us
    pallas_call x1, Pallas kernels, on_device(): local(final_kernel, (shape(here, width), shape(here, width)), [VMEM] * 2)  2.26 us

profile of v5, /device:TPU:1, one launch (start us, length us, event | category | flops | bytes accessed | tf_op | source)
XLA Modules:
  0.0 92.3 jit_solution(14138259067171830349)
XLA Ops:
  0.6 89.4 %shard_map.131 = (bf16[8,8,2,16,128]{4,3,2,1,0:T(8,128)(2,1)}, f32[256,128]{1,0:T(8,128)}) custom-call(f32[4]{0:T(128)} %slope_ref.1, bf16[256,256]{1,0:T(8,128)(2,1)} %pk_any.1, s32[256]{0:T(256)} %flow_any.1, s32[256]{0:T(256)} %pos_any.1, s32[256]{0:T(256)} %holder_any.1, s32[256]{0:T(256)} %first_any.1, bf16[256]{0:T(256)(128)(2,1)} %gain1_any.1, ...), custom_call_target="tpu_custom_call" | custom-call | tf_op jit(solution)/shard_map/pallas_call | solution.py:573
  90.1 2.3 %shard_map.132 = (bf16[256,256]{1,0:T(8,128)(2,1)}, bf16[256,256]{1,0:T(8,128)(2,1)}) custom-call(bf16[128,16,128]{2,1,0:T(8,128)(2,1)} %bitcast.1, f32[256,128]{1,0:T(8,128)} %get-tuple-element.5.rows_ref), custom_call_target="tpu_custom_call" | custom-call | tf_op jit(solution)/shard_map/pallas_call | solution.py:589

commit v6 on v5

--- a/solution.py
+++ b/solution.py
@@ -274,6 +274,7 @@
     a, b = spot.seen(core)
     oa, ob = spot.seen(other)
     rounds, few = 2, side // 2
+    far_first = sorted(range(1, side), key=lambda i: -min(i, side - i))
 
     barrier = pltpu.get_barrier_semaphore()
     friends = [spot.beside(1), spot.beside(-1), spot.device(core, a, b, other)]
@@ -319,7 +320,7 @@
                 remote(out_box.at[i, some], mid_ref.at[i, some], s1.at[h, i], r1.at[h, i],
                        spot.device(core, a + i, b, core))
             )
-            for i in range(1, side)
+            for i in far_first
         ]
 
     def hop2(h):
@@ -328,7 +329,7 @@
                 remote(mid_ref.at[:, h * few + i, t], in_box.at[h, t, i], s2.at[h, i, t], r2.at[h, i, t],
                        spot.device(core, a, b + h * few + i, core if t == 0 else other))
             )
-            for i in range(few) for t in range(2) if h or i or t
+            for i in (range(few) if h else reversed(range(few))) for t in range(2) if h or i or t
         ]
 
     first = [hop1(0), hop1(1)]
@@ -507,7 +508,7 @@
         for copy in third[h]:
             copy.wait_recv()
         some = pl.ds(h * few, few)
-        for i in range(1, side):
+        for i in far_first:
             fourth.append(
                 started(
                     remote(mid2_ref.at[i, some], back_ref.at[i, some], s4.at[h, i], r4.at[h, i],

time: 93.1 us -> 92.6 us (level)
  no operation moved by 1% of the time
where the time goes in v6:
time: 92.6 us; the launch traced here: 92.4 us
  Pallas kernels  91.8 us (99%)
    pallas_call x1, Pallas kernels, on_device(): linked(functools.partial(layer_kernel, side), (shape(*box), shape(here, 1...  89.5 us
    pallas_call x1, Pallas kernels, on_device(): local(final_kernel, (shape(here, width), shape(here, width)), [VMEM] * 2)  2.26 us

profile of v6, /device:TPU:1, one launch (start us, length us, event | category | flops | bytes accessed | tf_op | source)
XLA Modules:
  0.0 92.4 jit_solution(15358976235848037002)
XLA Ops:
  0.6 89.5 %shard_map.131 = (bf16[8,8,2,16,128]{4,3,2,1,0:T(8,128)(2,1)}, f32[256,128]{1,0:T(8,128)}) custom-call(f32[4]{0:T(128)} %slope_ref.1, bf16[256,256]{1,0:T(8,128)(2,1)} %pk_any.1, s32[256]{0:T(256)} %flow_any.1, s32[256]{0:T(256)} %pos_any.1, s32[256]{0:T(256)} %holder_any.1, s32[256]{0:T(256)} %first_any.1, bf16[256]{0:T(256)(128)(2,1)} %gain1_any.1, ...), custom_call_target="tpu_custom_call" | custom-call | tf_op jit(solution)/shard_map/pallas_call | solution.py:574
  90.2 2.3 %shard_map.132 = (bf16[256,256]{1,0:T(8,128)(2,1)}, bf16[256,256]{1,0:T(8,128)(2,1)}) custom-call(bf16[128,16,128]{2,1,0:T(8,128)(2,1)} %bitcast.1, f32[256,128]{1,0:T(8,128)} %get-tuple-element.5.rows_ref), custom_call_target="tpu_custom_call" | custom-call | tf_op jit(solution)/shard_map/pallas_call | solution.py:590
